TPU v7x, 32 devices: a whole 2x2x4 slice. The times are simulated.
32 devices in a mesh: seq: 8 (over z, x), head: 4 (over y, core).
Axes of the slice: x: 2, y: 2, z: 4, core: 2. Of those that a mesh axis runs over, the one named last changes fastest.
Arguments:
- qkv_tokens: bfloat16 [2, 3072, 3, 4096], P(None, ('seq', 'head')), may hold values from -6 to 6
- sign_bits: int32 [32, 2, 3, 128], P('head'), may hold values from 0 to 1
- out_weight: bfloat16 [4096, 4096], P('head'), may hold values from -0.09375 to 0.09375
Outputs:
- layer_out: bfloat16 [2, 3072, 4096], P(None, ('seq', 'head'))
Inputs may be any that keep to these rules, and one draw needn't show every extreme that they name: `sign_bits`: 1 stands for the sign +1 and 0 for -1.
All inputs are finite; a program needn't handle non-finite values.
Results may differ from a plain program's by a relative error of at most 0.014.
Values may be sent and summed in bfloat16 or wider, within the bound.
No kernel may reach another device: no remote copies, remote signals or barrier semaphores. Data moves between devices by JAX's collectives and lax.ppermute only.
A program may use at most 256 MiB of HBM per device.

v0:
```python
import functools
import math

import jax
import jax.numpy as jnp
import numpy as np
from jax import lax
from jax.experimental import pallas as pl
from jax.experimental.pallas import tpu as pltpu
from jax.sharding import PartitionSpec as P

logit_divisor = 1.3
norm_epsilon = 1e-06
SLABS = (8,), (4, 3, 1)

bf16, f32 = jnp.bfloat16, jnp.float32
ROW_TILE = 16
STEP_US = 4
GROUP = 4


def params(mebibytes=20):
    return pltpu.CompilerParams(vmem_limit_bytes=mebibytes * 1024 * 1024)


def vmem(count):
    return [pl.BlockSpec(memory_space=pltpu.VMEM)] * count


def smem():
    return pl.BlockSpec(memory_space=pltpu.SMEM)


def ordered(kernel, count, skip):
    return lambda *refs: kernel(*refs[:skip], *refs[skip + count :])


def busy(microseconds):
    return pl.CostEstimate(flops=int(microseconds * 1e9), bytes_accessed=0, transcendentals=0)


def waits(after):
    return [pl.BlockSpec(memory_space=pl.ANY)] * len(after)


def swap(value, axis, bit):
    return lax.ppermute(value, axis, [(j, j ^ bit) for j in range(lax.axis_size(axis))])


def sign_matrix(order):
    ids = np.arange(order)
    common = ids[:, None] & ids[None, :]
    parity = np.zeros_like(common)
    while common.any():
        parity ^= common & 1
        common = common >> 1
    return (1 - 2 * parity).astype(np.float32)


def maps_kernel(bits_ref, had_ref, maps_ref):
    had = had_ref[...]
    dh = had.shape[0]
    for h in range(bits_ref.shape[0]):
        for b in range(bits_ref.shape[1]):
            signs = (2 * bits_ref[h, b] - 1).astype(f32)
            inner = jnp.dot((had * signs[2:3]).astype(bf16), had, preferred_element_type=f32)
            outer = jnp.dot((inner * signs[1:2]).astype(bf16), had, preferred_element_type=f32)
            whole = outer * signs[0:1]
            near = whole.astype(bf16)
            rows = slice(b * dh, (b + 1) * dh)
            maps_ref[h, rows, :dh] = near
            maps_ref[h, rows, dh:] = (whole - near.astype(f32)).astype(bf16)


def integer_maps(sign_bits):
    heads, blocks, _, dh = sign_bits.shape
    return pl.pallas_call(
        maps_kernel,
        out_shape=jax.ShapeDtypeStruct((heads, blocks * dh, 2 * dh), bf16),
        in_specs=vmem(2),
        out_specs=vmem(1)[0],
        compiler_params=params(),
        cost_estimate=busy(0),
        name="integer_maps",
    )(sign_bits, jnp.asarray(sign_matrix(dh), bf16))


def features(rows_of, maps_ref, out_ref):
    heads, _, twice = maps_ref.shape
    dh = twice // 2
    rows = [rows_of(i) for i in range(heads)]
    scales = []
    for i in range(heads):
        wide = rows[i].astype(f32)
        mean = jnp.sum(wide * wide, axis=-1, keepdims=True) * (1.0 / dh)
        scales.append(lax.rsqrt(mean + norm_epsilon) * (logit_divisor / dh**0.25 / dh))
    for i in range(heads):
        product = lax.dot_general(
            jnp.concatenate([rows[i], rows[i]], axis=1),
            maps_ref[i],
            (((1,), (1,)), ((), ())),
            preferred_element_type=f32,
        )
        out_ref[i] = jnp.exp(product * scales[i]).astype(bf16)


def pack_kernel(places, arrays, where_ref, *refs):
    ins, outs, sems = refs[:arrays], refs[arrays:-1], refs[-1]
    copies = []
    for n, (which, first, second, k, out, i, j, count) in enumerate(places):
        width = outs[out].shape[-1]
        start = 0 if k is None else pl.multiple_of((where_ref[0] ^ k) * width, width)
        source = ins[which].at[first, pl.ds(second, count), :, pl.ds(start, width)]
        copies.append(pltpu.make_async_copy(source, outs[out].at[i, pl.ds(j, count)], sems.at[n]))
    for copy in copies:
        copy.start()
    for copy in copies:
        copy.wait()


def pack(where, wanted, shape, mebibytes):
    arrays, places, shapes = [], [], []
    for out, table in enumerate(wanted):
        shapes.append((len(table), len(table[0]), *shape))
        for i, row in enumerate(table):
            for j, (array, first, second, k) in enumerate(row):
                if not any(array is known for known in arrays):
                    arrays.append(array)
                which = [array is known for known in arrays].index(True)
                before = places[-1] if places else None
                if before and before[:6] == (which, first, second - before[7], k, out, i):
                    places[-1] = (*before[:7], before[7] + 1)
                else:
                    places.append((which, first, second, k, out, i, j, 1))
    return pl.pallas_call(
        functools.partial(pack_kernel, places, len(arrays)),
        out_shape=[jax.ShapeDtypeStruct(shape, bf16) for shape in shapes],
        in_specs=[pl.BlockSpec(memory_space=pltpu.SMEM)]
        + [pl.BlockSpec(memory_space=pl.ANY)] * len(arrays),
        out_specs=[pl.BlockSpec(memory_space=pltpu.VMEM)] * len(shapes),
        scratch_shapes=[pltpu.SemaphoreType.DMA((len(places),))],
        compiler_params=params(mebibytes),
        cost_estimate=busy(0),
        name="pack",
    )(where, *arrays)


def joined(refs, places, cut):
    return jnp.concatenate(
        [ref[lead, kind, :, cut] for ref, (lead, kind) in zip(refs, places)], axis=0
    )


def sums_kernel(k_at, v_at, heads, dh, maps_ref, *refs):
    pieces = len(k_at)
    k_refs, v_refs = refs[:pieces], refs[pieces : 2 * pieces]
    *before, feats_ref, sums_ref = refs[2 * pieces :]
    cuts = [slice(i * dh, (i + 1) * dh) for i in range(heads)]
    features(lambda i: joined(k_refs, k_at, cuts[i]), maps_ref, feats_ref)
    for i in range(heads):
        feats = feats_ref[i]
        state = lax.dot_general(
            joined(v_refs, v_at, cuts[i]),
            feats,
            (((0,), (0,)), ((), ())),
            preferred_element_type=f32,
        )
        sums_ref[i, :dh] = before[0][i, :dh] + state if before else state
    for i in range(heads):
        total = jnp.sum(feats_ref[i].astype(f32), axis=0, keepdims=True)
        total = jnp.broadcast_to(total, (sums_ref.shape[1] - dh, total.shape[1]))
        sums_ref[i, dh:] = before[0][i, dh:] + total if before else total


def early_sums(maps, keys, values, heads, dh, piece, after):
    feat = maps.shape[1]
    rows = len(keys) * piece
    (arrays, k_at), (others, v_at) = split(keys), split(values)
    return pl.pallas_call(
        ordered(functools.partial(sums_kernel, k_at, v_at, heads, dh), len(after), 0),
        out_shape=[
            jax.ShapeDtypeStruct((heads, rows, feat), bf16),
            jax.ShapeDtypeStruct((heads, dh + 8, feat), f32),
        ],
        in_specs=waits(after) + vmem(1 + 2 * len(keys)),
        out_specs=vmem(2),
        compiler_params=params(),
        cost_estimate=busy(0),
        name="early_sums",
    )(*after, maps, *arrays, *others)


def split(pieces):
    return [piece[0] for piece in pieces], [piece[1:] for piece in pieces]


def state_kernel(k_at, v_at, heads, dh, where_ref, maps_ref, *refs):
    count = 2 * len(k_at) + 2
    *ins, feats_ref, sums_ref = refs[:count] + refs[-1:]
    share_refs = refs[count:-1]
    sums_kernel(k_at, v_at, heads, dh, maps_ref, *ins, feats_ref, sums_ref)
    share = heads // GROUP
    pad = jnp.zeros((ROW_TILE - share, feats_ref.shape[-1]), f32)
    states = [sums_ref[i] for i in range(heads)]
    shares = []
    for g in range(GROUP):
        mine = states[g * share : (g + 1) * share]
        shares.append(
            jnp.concatenate([v[:dh] for v in mine] + [v[dh : dh + 1] for v in mine] + [pad], axis=0)
        )
    for m, ref in enumerate(share_refs):
        ref[...] = chosen(shares, where_ref[1] ^ m).astype(ref.dtype)


def chosen(values, index):
    result = values[0]
    for n, value in enumerate(values[1:]):
        result = jnp.where(index == n + 1, value, result)
    return result


def block_state(where, maps, keys, values, before, heads, dh, piece, after, beside):
    feat = maps.shape[1]
    rows = len(keys) * piece
    height = heads // GROUP * dh + ROW_TILE
    (arrays, k_at), (others, v_at) = split(keys), split(values)
    return pl.pallas_call(
        ordered(functools.partial(state_kernel, k_at, v_at, heads, dh), len(after), 0),
        out_shape=[
            jax.ShapeDtypeStruct((heads, rows, feat), bf16),
            jax.ShapeDtypeStruct((height, feat), f32),
        ]
        + [jax.ShapeDtypeStruct((height, feat), bf16)] * (GROUP - 1),
        in_specs=waits(after) + [smem()] + vmem(2 + 2 * len(keys)),
        out_specs=vmem(1 + GROUP),
        scratch_shapes=[pltpu.VMEM(before.shape, f32)],
        compiler_params=params(),
        cost_estimate=busy(beside),
        name="block_state",
    )(*after, where, maps, *arrays, *others, before)


def step_kernel(levels, where_ref, *refs):
    ins = refs[: len(refs) - (1 if len(refs) < 2 * GROUP + levels else GROUP)]
    outs = refs[len(ins) :]
    values = [ref[...].astype(f32) for ref in ins[:GROUP]]
    got = [ref[...].astype(f32) for ref in ins[GROUP:]]
    if len(outs) == 1:
        total = values[0]
        for value in values[1:] + got:
            total = total + value
        outs[0][...] = total.astype(bf16)
        return
    prior = jnp.zeros_like(values[0])
    for level, value in enumerate(got):
        prior = prior + jnp.where(where_ref[2 + level] == 1, value, 0.0)
    mine = where_ref[1]
    for m, out in enumerate(outs):
        result = prior
        for other, value in enumerate(values):
            if other != m:
                result = result + jnp.where((mine ^ other) < (mine ^ m), value, 0.0)
        out[...] = result.astype(bf16)


def chain_step(where, levels, values, after, beside):
    shape = values[0].shape
    count = GROUP if len(values) == GROUP + levels else 1
    return pl.pallas_call(
        ordered(functools.partial(step_kernel, levels), len(after), 0),
        out_shape=[jax.ShapeDtypeStruct(shape, bf16)] * count,
        in_specs=waits(after) + [smem()] + vmem(len(values)),
        out_specs=vmem(count),
        compiler_params=params(),
        cost_estimate=busy(beside),
        name="chain_step",
    )(*after, where, *values)


def local_kernel(first, q_at, v_at, heads, dh, where_ref, maps_ref, early_ref, late_ref, *refs):
    asking, partners = len(q_at), len(v_at)
    q_refs, v_refs = refs[:asking], refs[asking : asking + partners]
    query_feats_ref, local_ref, weights_ref = refs[asking + partners :]
    piece = q_refs[0].shape[2]
    rows = partners * piece
    me = where_ref[0]

    def places(first, count, shape, dim):
        ids = lax.broadcasted_iota(jnp.int32, shape, dim)
        result = ids + (me ^ first) * piece
        for j in range(1, count):
            result = jnp.where(ids >= j * piece, ids + ((me ^ (first + j)) - j) * piece, result)
        return result

    here = places(first, asking, (asking * piece, 1), 0)
    causal = here >= places(0, partners, (1, rows), 1)
    ones = jnp.ones((rows, dh), bf16)
    cuts = [slice(i * dh, (i + 1) * dh) for i in range(heads)]
    features(lambda i: joined(q_refs, q_at, cuts[i]), maps_ref, query_feats_ref)
    for i in range(heads):
        scores = lax.dot_general(
            query_feats_ref[i],
            jnp.concatenate([early_ref[i], late_ref[i]], axis=0),
            (((1,), (1,)), ((), ())),
            preferred_element_type=f32,
        )
        weights_ref[i] = jnp.where(causal, scores, 0.0).astype(bf16)
    for i in range(heads):
        local_ref[i] = jnp.dot(
            weights_ref[i],
            jnp.concatenate([joined(v_refs, v_at, cuts[i]), ones], axis=1),
            preferred_element_type=f32,
        )


def attend_local(where, maps, feats, queries, values, first, heads, dh, piece, after, beside):
    feat = maps.shape[1]
    rows = len(queries) * piece
    (arrays, q_at), (others, v_at) = split(queries), split(values)
    return pl.pallas_call(
        ordered(functools.partial(local_kernel, first, q_at, v_at, heads, dh), len(after), 0),
        out_shape=[
            jax.ShapeDtypeStruct((heads, rows, feat), bf16),
            jax.ShapeDtypeStruct((heads, rows, 2 * dh), f32),
        ],
        in_specs=waits(after) + [smem()] + vmem(1 + len(feats) + len(queries) + len(values)),
        out_specs=vmem(2),
        scratch_shapes=[pltpu.VMEM((heads, rows, len(values) * piece), bf16)],
        compiler_params=params(),
        cost_estimate=busy(beside),
        name="attend_local",
    )(*after, where, maps, *feats, *arrays, *others)


def prior_kernel(pieces, heads, dh, where_ref, *refs):
    parts = len(pieces)
    asked = [(refs[2 * p], refs[2 * p + 1]) for p in range(parts)]
    share_refs, (stay_ref, leave_ref) = refs[2 * parts : 2 * parts + GROUP], refs[-2:]
    piece = stay_ref.shape[1]
    share = heads // GROUP
    priors = []
    for i in range(heads):
        j = i % share
        state, total = slice(j * dh, (j + 1) * dh), slice(share * dh, share * dh + ROW_TILE)
        source = where_ref[1] ^ (i // share)
        prior = chosen([ref[state, :] for ref in share_refs], source)
        tail = chosen([ref[total, :] for ref in share_refs], source)
        tail = jnp.broadcast_to(tail[j : j + 1, :], prior.shape)
        priors.append(jnp.concatenate([prior, tail], axis=0))
    first = 0
    for count, (query_feats_ref, local_ref) in zip(pieces, asked):
        sums = [
            local_ref[i]
            + lax.dot_general(
                query_feats_ref[i], priors[i], (((1,), (1,)), ((), ())), preferred_element_type=f32
            )
            for i in range(heads)
        ]
        for i in range(heads):
            attended = (sums[i][:, :dh] / sums[i][:, dh:]).astype(bf16)
            for n in range(count):
                out = leave_ref if (first + n) & 1 else stay_ref
                out[(first + n) // 2, :, i * dh : (i + 1) * dh] = attended[n * piece : (n + 1) * piece]
        first += count


def attend_prior(where, asked, shares, piece, dh, after, beside):
    heads = asked[0][0].shape[0]
    pieces = [query_feats.shape[1] // piece for query_feats, _ in asked]
    out = jax.ShapeDtypeStruct((sum(pieces) // 2, piece, heads * dh), bf16)
    values = [value for pair in asked for value in pair]
    return pl.pallas_call(
        ordered(functools.partial(prior_kernel, pieces, heads, dh), len(after), 0),
        out_shape=[out, out],
        in_specs=waits(after) + [smem()] + vmem(len(values) + len(shares)),
        out_specs=vmem(2),
        compiler_params=params(),
        cost_estimate=busy(beside),
        name="attend_prior",
    )(*after, where, *values, *shares)


def project_kernel(parts, *refs):
    own_refs, other_refs = refs[:parts], refs[parts : 2 * parts]
    own_w, other_w, stay_ref, *leave_refs = refs[2 * parts :]
    groups, piece, width = own_refs[0].shape
    acc = None
    for lhs_refs, w_ref in ((own_refs, own_w), (other_refs, other_w)):
        for p, ref in enumerate(lhs_refs):
            lhs = ref[...].reshape(groups * piece, width)
            term = jnp.dot(
                lhs, w_ref[p * width : (p + 1) * width, :], preferred_element_type=f32
            )
            acc = term if acc is None else acc + term
    stay_ref[...] = acc[:piece]
    for g, ref in enumerate(leave_refs):
        ref[...] = acc[(g + 1) * piece : (g + 2) * piece].astype(bf16)


def project(own, other, own_w, other_w, slabs, slab, after, beside):
    parts, (groups, piece, width) = len(own), own[0].shape
    depth, cols = own_w.shape
    unit = cols // sum(slabs)
    tile = math.gcd(cols * slabs[slab] // sum(slabs), 1024)
    tile = math.gcd(tile, sum(slabs[:slab]) * unit) if slab else tile
    first, cols = sum(slabs[:slab]) * unit // tile, slabs[slab] * unit
    lhs = pl.BlockSpec((groups, piece, width), lambda n: (0, 0, 0))
    weight = pl.BlockSpec((depth, tile), lambda n: (0, first + n))
    out = pl.BlockSpec((piece, tile), lambda n: (0, n))
    return pl.pallas_call(
        ordered(functools.partial(project_kernel, parts), len(after), 0),
        grid=(cols // tile,),
        out_shape=[jax.ShapeDtypeStruct((piece, cols), f32)]
        + [jax.ShapeDtypeStruct((piece, cols), bf16)] * (groups - 1),
        in_specs=waits(after) + [lhs] * (2 * parts) + [weight, weight],
        out_specs=[out] * groups,
        compiler_params=params(),
        cost_estimate=busy(beside),
        name="project",
    )(*after, *own, *other, own_w, other_w)


def finish_kernel(counts, *refs):
    refs = list(refs)
    out_ref = refs.pop()
    for s, slabs in enumerate(counts):
        at = 0
        for shares in slabs:
            total = refs.pop(0)[...]
            for _ in range(shares):
                total = total + refs.pop(0)[...].astype(f32)
            width = total.shape[1]
            out_ref[s, :, at : at + width] = total.astype(bf16)
            at += width


def finish(sums, piece):
    *slabs, (total, shares) = sums[-1]
    most = [*sums[:-1], slabs]
    counts = [[len(given) for _, given in row] for row in most]
    values = [value for row in most for own, given in row for value in (own, *given)]
    out = jax.ShapeDtypeStruct(
        (len(sums), piece, sum(own.shape[1] for own, _ in sums[-1])), bf16
    )
    begun = pl.pallas_call(
        functools.partial(finish_kernel, counts),
        grid=(1,),
        out_shape=out,
        in_specs=[pl.BlockSpec(value.shape, lambda _: (0, 0)) for value in values],
        out_specs=pl.BlockSpec(out.shape, lambda _: (0, 0, 0)),
        compiler_params=params(),
        cost_estimate=busy(3),
        name="finish",
    )(*values)
    width = total.shape[1]
    place = (len(sums) - 1, 0, out.shape[2] // width - 1)
    return pl.pallas_call(
        ordered(functools.partial(finish_kernel, [[len(shares)]]), 1, 0),
        grid=(1,),
        out_shape=out,
        in_specs=waits([begun])
        + [pl.BlockSpec(value.shape, lambda _: (0, 0)) for value in (total, *shares)],
        out_specs=pl.BlockSpec((1, piece, width), lambda _: place),
        input_output_aliases={0: 0},
        compiler_params=params(),
        cost_estimate=busy(0),
        name="finish_last",
    )(begun, total, *shares)


def nothing(*refs):
    pass


def later_than(value, after):
    anywhere = pl.BlockSpec(memory_space=pl.ANY)
    return pl.pallas_call(
        nothing,
        out_shape=jax.ShapeDtypeStruct(value.shape, value.dtype),
        in_specs=[anywhere] * (1 + len(after)),
        out_specs=anywhere,
        input_output_aliases={0: 0},
        compiler_params=params(1),
        cost_estimate=busy(0),
        name="later_than",
    )(value, *after)


def body(qkv_tokens, sign_bits, out_weight):
    partners, blocks = lax.axis_size("head"), lax.axis_size("seq")
    me, index = lax.axis_index("head"), lax.axis_index("seq")
    seqs = qkv_tokens.shape[0]
    heads, dh = sign_bits.shape[0], sign_bits.shape[-1]
    levels = (blocks // GROUP).bit_length() - 1
    x = qkv_tokens.transpose(0, 2, 1, 3)
    piece = x.shape[2]
    where = jnp.stack(
        [me, index % GROUP] + [(index // GROUP >> l) & 1 for l in range(levels)]
    ).astype(jnp.int32)

    outer, shape = range(2, partners, 2), (piece, x.shape[3] // partners)
    beside = [(s, kind, 1) for s in range(seqs) for kind in (0, 1, 2)]
    beside += [
        (s, kind, k + 1)
        for s in range(seqs)
        for kind in (0, 1, 2)
        for k in outer
        if s > 0 or kind == 0
    ]
    straight = [[[(x, 0, kind, k) for kind in (1, 2)]] for k in range(2, partners)]
    *first, near = pack(where, [*straight, [[(x, *entry) for entry in beside]]], shape, 60)
    first = [swap(value, "head", k + 2) for k, value in enumerate(first)]
    near = swap(near, "head", 1)
    messages = [(s, (1, 2)) for s in range(1, seqs)] + [(s, (0,)) for s in range(seqs)]
    wanted = [
        [
            [(x, s, kind, k) for kind in kinds],
            [(near, 0, beside.index((s, kind, k + 1)), None) for kind in kinds],
        ]
        for s, kinds in messages
        for k in outer
    ]
    wanted.append([[(x, s, kind, 0) for kind in (0, 1, 2)] for s in range(seqs)])
    *packed, own_rows = pack(where, wanted, shape, 20)
    packed = [swap(value, "head", k) for value, k in zip(packed, list(outer) * len(messages))]
    packed = [packed[n * len(outer) : (n + 1) * len(outer)] for n in range(len(messages))]
    asked = packed[seqs - 1 :]

    def pieces(s, kind):
        found = [(own_rows, s, kind), (near, 0, beside.index((s, kind, 1)))]
        if s == 0 and kind > 0:
            return found + [(value, 0, kind - 1) for value in first]
        row, at = (packed[s - 1], kind - 1) if kind > 0 else (asked[s], 0)
        return found + [(value, half, at) for value in row for half in (0, 1)]

    maps = integer_maps(sign_bits)

    last = [own_rows]
    begun, chains, ends, locals_, own, other, totals = {}, {}, {}, {}, {}, {}, {}

    def early(n):
        begun[n] = early_sums(
            maps, pieces(n, 1)[:2], pieces(n, 2)[:2], heads, dh, piece, last
        )
        last[:] = [begun[n][0]]

    def state(n):
        feats, mine, *others = block_state(
            where,
            maps,
            pieces(n, 1)[2:],
            pieces(n, 2)[2:],
            begun[n][1],
            heads,
            dh,
            piece,
            last,
            3 if n else 0,
        )
        begun[n] = begun[n][0], feats
        chains[n] = [mine] + [swap(value, "seq", m + 1) for m, value in enumerate(others)]
        last[:] = [mine]

    def step(n):
        first_out, *others = chain_step(where, levels, chains[n], last, STEP_US if n and len(chains[n]) == GROUP else 0)
        last[:] = [first_out]
        if others:
            ends[n] = [first_out] + [swap(value, "seq", m + 1) for m, value in enumerate(others)]
        else:
            chains[n] = chains[n] + [swap(first_out, "seq", GROUP << (len(chains[n]) - GROUP))]

    def local(n, first, last_row):
        part = attend_local(
            where,
            maps,
            begun[n],
            pieces(n, 0)[first:last_row],
            pieces(n, 2),
            first,
            heads,
            dh,
            piece,
            last,
            3,
        )
        locals_.setdefault(n, []).append(part)
        last[:] = [part[0]]

    def attend(n):
        stay, leave = attend_prior(
            where, locals_[n], ends[n], piece, dh, last, 1 if n + 1 < seqs else 0
        )
        own[n], other[n] = [stay], [swap(leave, "head", 1)]
        last[:] = [stay]

    def multiply(s, slab):
        if slab == 1:
            for key in totals:
                if key[0] < s:
                    last.extend(totals[key][1])
        total, *shares = project(
            own[s], other[s], out_weight, other_weight, slabs[s], slab, last, 0 if s == seqs - 1 else 6
        )
        totals[s, slab] = total, [swap(v, "head", 2 * (g + 1)) for g, v in enumerate(shares)]
        last[:] = [total]

    slabs = [SLABS[0]] * (seqs - 1) + [SLABS[1]]
    plan = []
    for n in range(seqs):
        came = 22 * n
        end = came + 22 + 9 * levels
        plan.append((came, state, n))
        if n > 0:
            plan.append((came - 21, early, n))
        plan += [(came + 12 + 9 * j, step, n) for j in range(levels + 1)]
        if n == 0:
            plan += [(came + 12.5, local, n, 0, 2), (end - 7, local, n, 2, partners)]
        else:
            plan.append((end - 7, local, n, 0, partners))
        plan.append((end, attend, n))
        plan += [(end + 6 + 3.5 * j, multiply, n, j) for j in range(len(slabs[n]))]
    plan = sorted(plan, key=lambda entry: entry[0])
    early(0)
    state(0)
    other_weight = swap(later_than(out_weight, last), "head", 1)
    for _, act, *which in plan:
        if (act, which) != (state, [0]):
            act(*which)

    return finish([[totals[s, n] for n in range(len(slabs[s]))] for s in range(seqs)], piece)


def solution(mesh):
    return jax.shard_map(
        body,
        mesh=mesh,
        in_specs=(
            P(None, ("seq", "head"), None, None),
            P("head", None, None, None),
            P("head", None),
        ),
        out_specs=P(None, ("seq", "head"), None),
        check_vma=False,
    )
```

profile of v0, /device:TPU:0, one launch (start us, length us, event | category | flops | bytes accessed | tf_op | source)
XLA Modules:
  0.0 113.0 jit_solution(3939272160936266355)
XLA Ops:
  0.6 4.1 %pack.2 = (bf16[1,2,96,1024]{3,2,1,0:T(8,128)(2,1)}, bf16[1,2,96,1024]{3,2,1,0:T(8,128)(2,1)}, bf16[1,10,96,1024]{3,2,1,0:T(8,128)(2,1)}) custom-call(s32[3]{0:T(128)} %pad_add_fusion.where_ref.refs_1_, bf16[2,3,96,4096]{3,2,1,0:T(8,128)(2,1)} %bitcast.8), custom_call_target="tpu_custom_call" | custom-call | tf_op jit(solution)/shard_map/pack/pallas_call | solution.py:135
  5.2 2.6 %collective-permute-start.1 = (bf16[1,2,96,1024]{3,2,1,0:T(8,128)(2,1)}, bf16[1,2,96,1024]{3,2,1,0:T(8,128)(2,1)}, u32[]{:S(2)}, u32[]{:S(2)}) collective-permute-start(bf16[1,2,96,1024]{3,2,1,0:T(8,128)(2,1)} %get-tuple-element.55), channel_id=1, source_target_pairs={{0,2},{1,3},{2,0},{3,1},{4,6},{5,7},{6,4},{7,5},{8,10},{9,11},{10,... | collective-permute-start | bytes 1179656 | tf_op jit(solution)/shard_map/ppermute | solution.py:47
  7.9 7.9 %copy.8.refs_0_ = bf16[1024,4096]{1,0:T(8,128)(2,1)} copy(bf16[1024,4096]{1,0:T(8,128)(2,1)} %refs_3_.5) | data formatting | bytes 16777216
  19.7 6.3 %collective-permute-done.2.refs_4_.refs_6_.refs_10_ = bf16[1,2,96,1024]{3,2,1,0:T(8,128)(2,1)} collective-permute-done((bf16[1,2,96,1024]{3,2,1,0:T(8,128)(2,1)}, bf16[1,2,96,1024]{3,2,1,0:T(8,128)(2,1)}, u32[]{:S(2)}, u32[]{:S(2)}) %collective-permute-start.2) | collective-permute-done | bytes 393248 | tf_op jit(solution)/shard_map/ppermute | solution.py:47
  26.0 2.4 %block_state.2 = (bf16[8,192,256]{2,1,0:T(8,128)(2,1)S(1)}, f32[272,256]{1,0:T(8,128)S(1)}, bf16[272,256]{1,0:T(8,128)(2,1)S(1)}, bf16[272,256]{1,0:T(8,128)(2,1)S(1)}, bf16[272,256]{1,0:T(8,128)(2,1)S(1)}) custom-call(bf16[8,192,256]{2,1,0:T(8,128)(2,1)S(1)} %get-tuple-element.54.refs_0_.refs_3_, s32[3]{0:T(128)S(1)} %copy-done, ...), custom_call_target="tpu_custom_call" | custom-call | tf_op jit(solution)/shard_map/block_state/pallas_call | solution.py:227
  28.5 1.7 %collective-permute-start.7 = (bf16[2,2,96,1024]{3,2,1,0:T(8,128)(2,1)S(1)}, bf16[2,2,96,1024]{3,2,1,0:T(8,128)(2,1)S(1)}, u32[]{:S(2)}, u32[]{:S(2)}) collective-permute-start(bf16[2,2,96,1024]{3,2,1,0:T(8,128)(2,1)S(1)} %get-tuple-element.66), channel_id=1, source_target_pairs={{0,2},{1,3},{2,0},{3,1},{4,6},{5,7},{6,4},{7,5},{8,10},{9,11},{10,... | collective-permute-start | bytes 2359304 | tf_op jit(solution)/shard_map/ppermute | solution.py:47
  36.3 2.1 %collective-permute-done.4.refs_4_ = bf16[272,256]{1,0:T(8,128)(2,1)S(1)} collective-permute-done((bf16[272,256]{1,0:T(8,128)(2,1)S(1)}, bf16[272,256]{1,0:T(8,128)(2,1)S(1)}, u32[]{:S(2)}, u32[]{:S(2)}) %collective-permute-start.4) | collective-permute-done | bytes 139296 | tf_op jit(solution)/shard_map/ppermute | solution.py:47
  38.3 1.6 %collective-permute-done.5.refs_5_ = bf16[272,256]{1,0:T(8,128)(2,1)S(1)} collective-permute-done((bf16[272,256]{1,0:T(8,128)(2,1)S(1)}, bf16[272,256]{1,0:T(8,128)(2,1)S(1)}, u32[]{:S(2)}, u32[]{:S(2)}) %collective-permute-start.5) | collective-permute-done | bytes 139296 | tf_op jit(solution)/shard_map/ppermute | solution.py:47
  40.6 2.7 %collective-permute-start.6 = (bf16[272,256]{1,0:T(8,128)(2,1)S(1)}, bf16[272,256]{1,0:T(8,128)(2,1)S(1)}, u32[]{:S(2)}, u32[]{:S(2)}) collective-permute-start(bf16[272,256]{1,0:T(8,128)(2,1)S(1)} %chain_step.4.refs_0_), channel_id=1, source_target_pairs={{0,16},{4,20},{8,24},{12,28},{16,0},{20,4},{24,8},{28,12},{1,17},{... | collective-permute-start | bytes 417800 | tf_op jit(solution)/shard_map/ppermute | solution.py:47
  43.2 2.6 %attend_local.3 = (bf16[8,192,256]{2,1,0:T(8,128)(2,1)S(1)}, f32[8,192,256]{2,1,0:T(8,128)S(1)}) custom-call(bf16[272,256]{1,0:T(8,128)(2,1)S(1)} %chain_step.4.refs_0_, s32[3]{0:T(128)S(1)} %copy-done, bf16[8,256,256]{2,1,0:T(8,128)(2,1)S(1)} %integer_maps.1.refs_1_.refs_2_, bf16[8,192,256]{2,1,0:T(8,128)(2,1)S(1)} %get-tuple-element.54.refs_0_.refs_3_, ...), custom_call_target="tpu_custom_call" | custom-call | flops 3000000000 | tf_op jit(solution)/shard_map/attend_local/pallas_call | solution.py:320
  45.9 3.5 %collective-permute-done.6.refs_6_ = bf16[272,256]{1,0:T(8,128)(2,1)S(1)} collective-permute-done((bf16[272,256]{1,0:T(8,128)(2,1)S(1)}, bf16[272,256]{1,0:T(8,128)(2,1)S(1)}, u32[]{:S(2)}, u32[]{:S(2)}) %collective-permute-start.6) | collective-permute-done | bytes 139296 | tf_op jit(solution)/shard_map/ppermute | solution.py:47
  50.6 2.2 %collective-permute-start.11 = (bf16[272,256]{1,0:T(8,128)(2,1)S(1)}, bf16[272,256]{1,0:T(8,128)(2,1)S(1)}, u32[]{:S(2)}, u32[]{:S(2)}) collective-permute-start(bf16[272,256]{1,0:T(8,128)(2,1)S(1)} %get-tuple-element.75), channel_id=1, source_target_pairs={{0,12},{4,8},{8,4},{12,0},{16,28},{20,24},{24,20},{28,16},{1,13},{... | collective-permute-start | bytes 417800 | tf_op jit(solution)/shard_map/ppermute | solution.py:47
  60.3 2.6 %attend_local.4 = (bf16[8,192,256]{2,1,0:T(8,128)(2,1)S(1)}, f32[8,192,256]{2,1,0:T(8,128)S(1)}) custom-call(f32[272,256]{1,0:T(8,128)S(1)} %get-tuple-element.68.refs_0_.refs_2_, s32[3]{0:T(128)S(1)} %copy-done, bf16[8,256,256]{2,1,0:T(8,128)(2,1)S(1)} %integer_maps.1.refs_1_.refs_2_, bf16[8,192,256]{2,1,0:T(8,128)(2,1)S(1)} %get-tuple-element.54.refs_0_.refs_3_, ...), custom_call_target="tpu_custom_call" | custom-call | flops 3000000000 | tf_op jit(solution)/shard_map/attend_local/pallas_call | solution.py:320
  64.5 1.6 %collective-permute-start.19 = (bf16[2,1,96,1024]{3,2,1,0:T(8,128)(2,1)S(1)}, bf16[2,1,96,1024]{3,2,1,0:T(8,128)(2,1)S(1)}, u32[]{:S(2)}, u32[]{:S(2)}) collective-permute-start(bf16[2,1,96,1024]{3,2,1,0:T(8,128)(2,1)S(1)} %get-tuple-element.85), channel_id=1, source_target_pairs={{0,2},{1,3},{2,0},{3,1},{4,6},{5,7},{6,4},{7,5},{8,10},{9,11},{10,... | collective-permute-start | bytes 1179656 | tf_op jit(solution)/shard_map/ppermute | solution.py:47
  66.9 2.7 %collective-permute-start.18 = (bf16[272,256]{1,0:T(8,128)(2,1)S(1)}, bf16[272,256]{1,0:T(8,128)(2,1)S(1)}, u32[]{:S(2)}, u32[]{:S(2)}) collective-permute-start(bf16[272,256]{1,0:T(8,128)(2,1)S(1)} %chain_step.6.refs_0_), channel_id=1, source_target_pairs={{0,16},{4,20},{8,24},{12,28},{16,0},{20,4},{24,8},{28,12},{1,17},{... | collective-permute-start | bytes 417800 | tf_op jit(solution)/shard_map/ppermute | solution.py:47
  69.7 5.4 %project.4 = (f32[96,4096]{1,0:T(8,128)S(1)}, bf16[96,4096]{1,0:T(8,128)(2,1)S(1)}) custom-call(bf16[272,256]{1,0:T(8,128)(2,1)S(1)} %chain_step.6.refs_0_, bf16[2,96,1024]{2,1,0:T(8,128)(2,1)S(1)} %get-tuple-element.76.refs_0_.refs_1_, bf16[2,96,1024]{2,1,0:T(8,128)(2,1)S(1)} %collective-permute-done.15.refs_2_, bf16[1024,4096]{1,0:T(8,128)(2,1)S(1)} %bitcast.5, ...), custom_call_target="tpu_custom_call" | custom-call | flops 6000000000 | tf_op jit(solution)/shard_map/project/pallas_call | solution.py:410
  75.1 1.6 %collective-permute-start.17 = (bf16[96,4096]{1,0:T(8,128)(2,1)S(1)}, bf16[96,4096]{1,0:T(8,128)(2,1)S(1)}, u32[]{:S(2)}, u32[]{:S(2)}) collective-permute-start(bf16[96,4096]{1,0:T(8,128)(2,1)S(1)} %get-tuple-element.82), channel_id=1, source_target_pairs={{0,2},{1,3},{2,0},{3,1},{4,6},{5,7},{6,4},{7,5},{8,10},{9,11},{10,... | collective-permute-start | bytes 2359304 | tf_op jit(solution)/shard_map/ppermute | solution.py:47
  81.1 3.2 %attend_local.5 = (bf16[8,384,256]{2,1,0:T(8,128)(2,1)S(1)}, f32[8,384,256]{2,1,0:T(8,128)S(1)}) custom-call(bf16[272,256]{1,0:T(8,128)(2,1)S(1)} %get-tuple-element.83.refs_0_.refs_4_, s32[3]{0:T(128)S(1)} %copy-done, bf16[8,256,256]{2,1,0:T(8,128)(2,1)S(1)} %integer_maps.1.refs_1_.refs_2_, bf16[8,192,256]{2,1,0:T(8,128)(2,1)S(1)} %get-tuple-element.59.refs_0_.refs_3_, ...), custom_call_target="tpu_custom_call" | custom-call | flops 3000000000 | tf_op jit(solution)/shard_map/attend_local/pallas_call | solution.py:320
  85.0 2.0 %collective-permute-done.22.refs_7_ = bf16[272,256]{1,0:T(8,128)(2,1)S(1)} collective-permute-done((bf16[272,256]{1,0:T(8,128)(2,1)S(1)}, bf16[272,256]{1,0:T(8,128)(2,1)S(1)}, u32[]{:S(2)}, u32[]{:S(2)}) %collective-permute-start.22) | collective-permute-done | bytes 139296 | tf_op jit(solution)/shard_map/ppermute | solution.py:47
  88.2 1.7 %collective-permute-done.23.refs_2_.refs_3_ = bf16[2,96,1024]{2,1,0:T(8,128)(2,1)S(1)} collective-permute-done((bf16[2,96,1024]{2,1,0:T(8,128)(2,1)S(1)}, bf16[2,96,1024]{2,1,0:T(8,128)(2,1)S(1)}, u32[]{:S(2)}, u32[]{:S(2)}) %collective-permute-start.23) | collective-permute-done | bytes 393248 | tf_op jit(solution)/shard_map/ppermute | solution.py:47
  90.0 2.6 %project.5 = (f32[96,2048]{1,0:T(8,128)S(1)}, bf16[96,2048]{1,0:T(8,128)(2,1)S(1)}) custom-call(bf16[2,96,1024]{2,1,0:T(8,128)(2,1)S(1)} %get-tuple-element.91.refs_0_.refs_1_.refs_2_, bf16[2,96,1024]{2,1,0:T(8,128)(2,1)S(1)} %get-tuple-element.91.refs_0_.refs_1_.refs_2_, bf16[2,96,1024]{2,1,0:T(8,128)(2,1)S(1)} %collective-permute-done.23.refs_2_.refs_3_, ...), custom_call_target="tpu_custom_call" | custom-call | tf_op jit(solution)/shard_map/project/pallas_call | solution.py:410
  94.3 2.3 %project.6 = (f32[96,1536]{1,0:T(8,128)S(1)}, bf16[96,1536]{1,0:T(8,128)(2,1)S(1)}) custom-call(f32[96,2048]{1,0:T(8,128)S(1)} %get-tuple-element.93.refs_0_.refs_2_, bf16[96,4096]{1,0:T(8,128)(2,1)S(1)} %collective-permute-done.17.refs_1_, bf16[2,96,1024]{2,1,0:T(8,128)(2,1)S(1)} %get-tuple-element.91.refs_0_.refs_1_.refs_2_, ...), custom_call_target="tpu_custom_call" | custom-call | tf_op jit(solution)/shard_map/project/pallas_call | solution.py:410
  99.4 5.3 %collective-permute-done.24.refs_3_ = bf16[96,2048]{1,0:T(8,128)(2,1)S(1)} collective-permute-done((bf16[96,2048]{1,0:T(8,128)(2,1)S(1)}, bf16[96,2048]{1,0:T(8,128)(2,1)S(1)}, u32[]{:S(2)}, u32[]{:S(2)}) %collective-permute-start.24) | collective-permute-done | bytes 393248 | tf_op jit(solution)/shard_map/ppermute | solution.py:47
  104.6 6.3 %collective-permute-done.25.refs_5_ = bf16[96,1536]{1,0:T(8,128)(2,1)S(1)} collective-permute-done((bf16[96,1536]{1,0:T(8,128)(2,1)S(1)}, bf16[96,1536]{1,0:T(8,128)(2,1)S(1)}, u32[]{:S(2)}, u32[]{:S(2)}) %collective-permute-start.25) | collective-permute-done | bytes 294944 | tf_op jit(solution)/shard_map/ppermute | solution.py:47
  (77 shorter events, 35.6 us)
Async XLA Ops:
  4.7 12.5 %collective-permute-start = (bf16[1,10,96,1024]{3,2,1,0:T(8,128)(2,1)}, bf16[1,10,96,1024]{3,2,1,0:T(8,128)(2,1)S(1)}, u32[]{:S(2)}, u32[]{:S(2)}) collective-permute-start(bf16[1,10,96,1024]{3,2,1,0:T(8,128)(2,1)} %get-tuple-element.52), channel_id=1, source_target_pairs={{0,1},{1,0},{2,3},{3,2},{4,5},{5,4},{6,7},{7,6},{8,9},{9,8},{10,11... | collective-permute-start | bytes 5898248 | tf_op jit(solution)/shard_map/ppermute | solution.py:47
  5.2 14.5 %collective-permute-start.1 = (bf16[1,2,96,1024]{3,2,1,0:T(8,128)(2,1)}, bf16[1,2,96,1024]{3,2,1,0:T(8,128)(2,1)}, u32[]{:S(2)}, u32[]{:S(2)}) collective-permute-start(bf16[1,2,96,1024]{3,2,1,0:T(8,128)(2,1)} %get-tuple-element.55), channel_id=1, source_target_pairs={{0,2},{1,3},{2,0},{3,1},{4,6},{5,7},{6,4},{7,5},{8,10},{9,11},{10,... | collective-permute-start | bytes 1179656 | tf_op jit(solution)/shard_map/ppermute | solution.py:47
  7.8 18.2 %collective-permute-start.2 = (bf16[1,2,96,1024]{3,2,1,0:T(8,128)(2,1)}, bf16[1,2,96,1024]{3,2,1,0:T(8,128)(2,1)}, u32[]{:S(2)}, u32[]{:S(2)}) collective-permute-start(bf16[1,2,96,1024]{3,2,1,0:T(8,128)(2,1)} %get-tuple-element.56), channel_id=1, source_target_pairs={{0,3},{1,2},{2,1},{3,0},{4,7},{5,6},{6,5},{7,4},{8,11},{9,10},{10,... | collective-permute-start | bytes 1179656 | tf_op jit(solution)/shard_map/ppermute | solution.py:47
  28.4 41.3 %collective-permute-start.16 = (bf16[1024,4096]{1,0:T(8,128)(2,1)S(1)}, bf16[1024,4096]{1,0:T(8,128)(2,1)S(1)}, u32[]{:S(2)}, u32[]{:S(2)}) collective-permute-start(bf16[1024,4096]{1,0:T(8,128)(2,1)S(1)} %later_than.1), channel_id=1, source_target_pairs={{0,1},{1,0},{2,3},{3,2},{4,5},{5,4},{6,7},{7,6},{8,9},{9,8},{10,11... | collective-permute-start | bytes 25165832 | tf_op jit(solution)/shard_map/ppermute | solution.py:47
  28.5 24.2 %collective-permute-start.7 = (bf16[2,2,96,1024]{3,2,1,0:T(8,128)(2,1)S(1)}, bf16[2,2,96,1024]{3,2,1,0:T(8,128)(2,1)S(1)}, u32[]{:S(2)}, u32[]{:S(2)}) collective-permute-start(bf16[2,2,96,1024]{3,2,1,0:T(8,128)(2,1)S(1)} %get-tuple-element.66), channel_id=1, source_target_pairs={{0,2},{1,3},{2,0},{3,1},{4,6},{5,7},{6,4},{7,5},{8,10},{9,11},{10,... | collective-permute-start | bytes 2359304 | tf_op jit(solution)/shard_map/ppermute | solution.py:47
  31.8 6.6 %collective-permute-start.4 = (bf16[272,256]{1,0:T(8,128)(2,1)S(1)}, bf16[272,256]{1,0:T(8,128)(2,1)S(1)}, u32[]{:S(2)}, u32[]{:S(2)}) collective-permute-start(bf16[272,256]{1,0:T(8,128)(2,1)S(1)} %get-tuple-element.61), channel_id=1, source_target_pairs={{0,8},{4,12},{8,0},{12,4},{16,24},{20,28},{24,16},{28,20},{1,9},{5... | collective-permute-start | bytes 417800 | tf_op jit(solution)/shard_map/ppermute | solution.py:47
  33.3 6.6 %collective-permute-start.5 = (bf16[272,256]{1,0:T(8,128)(2,1)S(1)}, bf16[272,256]{1,0:T(8,128)(2,1)S(1)}, u32[]{:S(2)}, u32[]{:S(2)}) collective-permute-start(bf16[272,256]{1,0:T(8,128)(2,1)S(1)} %get-tuple-element.62), channel_id=1, source_target_pairs={{0,12},{4,8},{8,4},{12,0},{16,28},{20,24},{24,20},{28,16},{1,13},{... | collective-permute-start | bytes 417800 | tf_op jit(solution)/shard_map/ppermute | solution.py:47
  35.8 21.0 %collective-permute-start.8 = (bf16[2,1,96,1024]{3,2,1,0:T(8,128)(2,1)S(1)}, bf16[2,1,96,1024]{3,2,1,0:T(8,128)(2,1)S(1)}, u32[]{:S(2)}, u32[]{:S(2)}) collective-permute-start(bf16[2,1,96,1024]{3,2,1,0:T(8,128)(2,1)S(1)} %get-tuple-element.69), channel_id=1, source_target_pairs={{0,2},{1,3},{2,0},{3,1},{4,6},{5,7},{6,4},{7,5},{8,10},{9,11},{10,... | collective-permute-start | bytes 1179656 | tf_op jit(solution)/shard_map/ppermute | solution.py:47
  40.6 8.8 %collective-permute-start.6 = (bf16[272,256]{1,0:T(8,128)(2,1)S(1)}, bf16[272,256]{1,0:T(8,128)(2,1)S(1)}, u32[]{:S(2)}, u32[]{:S(2)}) collective-permute-start(bf16[272,256]{1,0:T(8,128)(2,1)S(1)} %chain_step.4.refs_0_), channel_id=1, source_target_pairs={{0,16},{4,20},{8,24},{12,28},{16,0},{20,4},{24,8},{28,12},{1,17},{... | collective-permute-start | bytes 417800 | tf_op jit(solution)/shard_map/ppermute | solution.py:47
  50.2 8.2 %collective-permute-start.10 = (bf16[272,256]{1,0:T(8,128)(2,1)S(1)}, bf16[272,256]{1,0:T(8,128)(2,1)S(1)}, u32[]{:S(2)}, u32[]{:S(2)}) collective-permute-start(bf16[272,256]{1,0:T(8,128)(2,1)S(1)} %get-tuple-element.74), channel_id=1, source_target_pairs={{0,8},{4,12},{8,0},{12,4},{16,24},{20,28},{24,16},{28,20},{1,9},{5... | collective-permute-start | bytes 417800 | tf_op jit(solution)/shard_map/ppermute | solution.py:47
  50.6 9.4 %collective-permute-start.11 = (bf16[272,256]{1,0:T(8,128)(2,1)S(1)}, bf16[272,256]{1,0:T(8,128)(2,1)S(1)}, u32[]{:S(2)}, u32[]{:S(2)}) collective-permute-start(bf16[272,256]{1,0:T(8,128)(2,1)S(1)} %get-tuple-element.75), channel_id=1, source_target_pairs={{0,12},{4,8},{8,4},{12,0},{16,28},{20,24},{24,20},{28,16},{1,13},{... | collective-permute-start | bytes 417800 | tf_op jit(solution)/shard_map/ppermute | solution.py:47
  52.8 10.2 %collective-permute-start.9 = (bf16[272,256]{1,0:T(8,128)(2,1)S(1)}, bf16[272,256]{1,0:T(8,128)(2,1)S(1)}, u32[]{:S(2)}, u32[]{:S(2)}) collective-permute-start(bf16[272,256]{1,0:T(8,128)(2,1)S(1)} %get-tuple-element.73), channel_id=1, source_target_pairs={{0,4},{4,0},{8,12},{12,8},{16,20},{20,16},{24,28},{28,24},{1,5},{5... | collective-permute-start | bytes 417800 | tf_op jit(solution)/shard_map/ppermute | solution.py:47
  56.8 7.7 %collective-permute-start.12 = (bf16[272,256]{1,0:T(8,128)(2,1)S(1)}, bf16[272,256]{1,0:T(8,128)(2,1)S(1)}, u32[]{:S(2)}, u32[]{:S(2)}) collective-permute-start(bf16[272,256]{1,0:T(8,128)(2,1)S(1)} %get-tuple-element.77), channel_id=1, source_target_pairs={{0,4},{4,0},{8,12},{12,8},{16,20},{20,16},{24,28},{28,24},{1,5},{5... | collective-permute-start | bytes 417800 | tf_op jit(solution)/shard_map/ppermute | solution.py:47
  58.4 7.8 %collective-permute-start.13 = (bf16[272,256]{1,0:T(8,128)(2,1)S(1)}, bf16[272,256]{1,0:T(8,128)(2,1)S(1)}, u32[]{:S(2)}, u32[]{:S(2)}) collective-permute-start(bf16[272,256]{1,0:T(8,128)(2,1)S(1)} %get-tuple-element.78), channel_id=1, source_target_pairs={{0,8},{4,12},{8,0},{12,4},{16,24},{20,28},{24,16},{28,20},{1,9},{5... | collective-permute-start | bytes 417800 | tf_op jit(solution)/shard_map/ppermute | solution.py:47
  59.9 6.4 %collective-permute-start.14 = (bf16[272,256]{1,0:T(8,128)(2,1)S(1)}, bf16[272,256]{1,0:T(8,128)(2,1)S(1)}, u32[]{:S(2)}, u32[]{:S(2)}) collective-permute-start(bf16[272,256]{1,0:T(8,128)(2,1)S(1)} %get-tuple-element.79), channel_id=1, source_target_pairs={{0,12},{4,8},{8,4},{12,0},{16,28},{20,24},{24,20},{28,16},{1,13},{... | collective-permute-start | bytes 417800 | tf_op jit(solution)/shard_map/ppermute | solution.py:47
  64.5 16.6 %collective-permute-start.19 = (bf16[2,1,96,1024]{3,2,1,0:T(8,128)(2,1)S(1)}, bf16[2,1,96,1024]{3,2,1,0:T(8,128)(2,1)S(1)}, u32[]{:S(2)}, u32[]{:S(2)}) collective-permute-start(bf16[2,1,96,1024]{3,2,1,0:T(8,128)(2,1)S(1)} %get-tuple-element.85), channel_id=1, source_target_pairs={{0,2},{1,3},{2,0},{3,1},{4,6},{5,7},{6,4},{7,5},{8,10},{9,11},{10,... | collective-permute-start | bytes 1179656 | tf_op jit(solution)/shard_map/ppermute | solution.py:47
  66.9 9.8 %collective-permute-start.18 = (bf16[272,256]{1,0:T(8,128)(2,1)S(1)}, bf16[272,256]{1,0:T(8,128)(2,1)S(1)}, u32[]{:S(2)}, u32[]{:S(2)}) collective-permute-start(bf16[272,256]{1,0:T(8,128)(2,1)S(1)} %chain_step.6.refs_0_), channel_id=1, source_target_pairs={{0,16},{4,20},{8,24},{12,28},{16,0},{20,4},{24,8},{28,12},{1,17},{... | collective-permute-start | bytes 417800 | tf_op jit(solution)/shard_map/ppermute | solution.py:47
  75.1 19.2 %collective-permute-start.17 = (bf16[96,4096]{1,0:T(8,128)(2,1)S(1)}, bf16[96,4096]{1,0:T(8,128)(2,1)S(1)}, u32[]{:S(2)}, u32[]{:S(2)}) collective-permute-start(bf16[96,4096]{1,0:T(8,128)(2,1)S(1)} %get-tuple-element.82), channel_id=1, source_target_pairs={{0,2},{1,3},{2,0},{3,1},{4,6},{5,7},{6,4},{7,5},{8,10},{9,11},{10,... | collective-permute-start | bytes 2359304 | tf_op jit(solution)/shard_map/ppermute | solution.py:47
  77.5 6.7 %collective-permute-start.20 = (bf16[272,256]{1,0:T(8,128)(2,1)S(1)}, bf16[272,256]{1,0:T(8,128)(2,1)S(1)}, u32[]{:S(2)}, u32[]{:S(2)}) collective-permute-start(bf16[272,256]{1,0:T(8,128)(2,1)S(1)} %get-tuple-element.88), channel_id=1, source_target_pairs={{0,4},{4,0},{8,12},{12,8},{16,20},{20,16},{24,28},{28,24},{1,5},{5... | collective-permute-start | bytes 417800 | tf_op jit(solution)/shard_map/ppermute | solution.py:47
  78.8 6.1 %collective-permute-start.21 = (bf16[272,256]{1,0:T(8,128)(2,1)S(1)}, bf16[272,256]{1,0:T(8,128)(2,1)S(1)}, u32[]{:S(2)}, u32[]{:S(2)}) collective-permute-start(bf16[272,256]{1,0:T(8,128)(2,1)S(1)} %get-tuple-element.89), channel_id=1, source_target_pairs={{0,8},{4,12},{8,0},{12,4},{16,24},{20,28},{24,16},{28,20},{1,9},{5... | collective-permute-start | bytes 417800 | tf_op jit(solution)/shard_map/ppermute | solution.py:47
  80.3 6.6 %collective-permute-start.22 = (bf16[272,256]{1,0:T(8,128)(2,1)S(1)}, bf16[272,256]{1,0:T(8,128)(2,1)S(1)}, u32[]{:S(2)}, u32[]{:S(2)}) collective-permute-start(bf16[272,256]{1,0:T(8,128)(2,1)S(1)} %get-tuple-element.90), channel_id=1, source_target_pairs={{0,12},{4,8},{8,4},{12,0},{16,28},{20,24},{24,20},{28,16},{1,13},{... | collective-permute-start | bytes 417800 | tf_op jit(solution)/shard_map/ppermute | solution.py:47
  92.6 12.0 %collective-permute-start.24 = (bf16[96,2048]{1,0:T(8,128)(2,1)S(1)}, bf16[96,2048]{1,0:T(8,128)(2,1)S(1)}, u32[]{:S(2)}, u32[]{:S(2)}) collective-permute-start(bf16[96,2048]{1,0:T(8,128)(2,1)S(1)} %get-tuple-element.94), channel_id=1, source_target_pairs={{0,2},{1,3},{2,0},{3,1},{4,6},{5,7},{6,4},{7,5},{8,10},{9,11},{10,... | collective-permute-start | bytes 1179656 | tf_op jit(solution)/shard_map/ppermute | solution.py:47
  96.6 14.3 %collective-permute-start.25 = (bf16[96,1536]{1,0:T(8,128)(2,1)S(1)}, bf16[96,1536]{1,0:T(8,128)(2,1)S(1)}, u32[]{:S(2)}, u32[]{:S(2)}) collective-permute-start(bf16[96,1536]{1,0:T(8,128)(2,1)S(1)} %get-tuple-element.96), channel_id=1, source_target_pairs={{0,2},{1,3},{2,0},{3,1},{4,6},{5,7},{6,4},{7,5},{8,10},{9,11},{10,... | collective-permute-start | bytes 884744 | tf_op jit(solution)/shard_map/ppermute | solution.py:47
  97.8 14.5 %collective-permute-start.26 = (bf16[96,512]{1,0:T(8,128)(2,1)S(1)}, bf16[96,512]{1,0:T(8,128)(2,1)S(1)}, u32[]{:S(2)}, u32[]{:S(2)}) collective-permute-start(bf16[96,512]{1,0:T(8,128)(2,1)S(1)} %get-tuple-element.98), channel_id=1, source_target_pairs={{0,2},{1,3},{2,0},{3,1},{4,6},{5,7},{6,4},{7,5},{8,10},{9,11},{10,... | collective-permute-start | bytes 294920 | tf_op jit(solution)/shard_map/ppermute | solution.py:47
  (12 other events, 79.3 us)
where the time goes:
time: 113 us
  Pallas kernels  38.9 us (34%)
  waiting for transfers between devices  33.3 us (29%)
  starting transfers between devices  31.2 us (28%)
  local copies, waits for them, and re-layouts  8.75 us (8%)
    ppermute x27, waiting for transfers between devices, swap(): lax.ppermute(value, axis, [(j, j ^ bit) for j in range(lax.axis_size(axis...  33.3 us
    ppermute x27, starting transfers between devices, swap(): lax.ppermute(value, axis, [(j, j ^ bit) for j in range(lax.axis_size(axis...  31.2 us
    pallas_call x4, Pallas kernels, project(): pl.pallas_call(ordered(functools.partial(project_kernel, parts), len(afte...  11 us
    unnamed x20, local copies, waits for them, and re-layouts  8.75 us
    pallas_call x3, Pallas kernels, attend_local(): pl.pallas_call(ordered(functools.partial(local_kernel, first, q_at, v_at,...  8.45 us
    pallas_call x2, Pallas kernels, pack(): pl.pallas_call(functools.partial(pack_kernel, places, len(arrays)), out_s...  5.62 us
    pallas_call x2, Pallas kernels, block_state(): pl.pallas_call(ordered(functools.partial(state_kernel, k_at, v_at, heads,...  3.88 us
    pallas_call x4, Pallas kernels, chain_step(): pl.pallas_call(ordered(functools.partial(step_kernel, levels), len(after)...  2.88 us
  transfers between devices with their start and end apart: 27, of which 13 were waited for; matrix products, arithmetic and copies ran while one was open for 7% of the time, Pallas kernels for 28%

commit v1 on v0

--- a/solution.py
+++ b/solution.py
@@ -380,44 +380,36 @@
     )(*after, where, *values, *shares)
 
 
-def project_kernel(parts, *refs):
-    own_refs, other_refs = refs[:parts], refs[parts : 2 * parts]
-    own_w, other_w, stay_ref, *leave_refs = refs[2 * parts :]
-    groups, piece, width = own_refs[0].shape
-    acc = None
-    for lhs_refs, w_ref in ((own_refs, own_w), (other_refs, other_w)):
-        for p, ref in enumerate(lhs_refs):
-            lhs = ref[...].reshape(groups * piece, width)
-            term = jnp.dot(
-                lhs, w_ref[p * width : (p + 1) * width, :], preferred_element_type=f32
-            )
-            acc = term if acc is None else acc + term
-    stay_ref[...] = acc[:piece]
-    for g, ref in enumerate(leave_refs):
-        ref[...] = acc[(g + 1) * piece : (g + 2) * piece].astype(bf16)
+def project_kernel(first, tile, own_ref, other_ref, own_w, other_w, stay_ref, *leave_refs):
+    groups, piece, width = own_ref.shape
+    lhs = [ref[...].reshape(groups * piece, width) for ref in (own_ref, other_ref)]
+    for n in range(stay_ref.shape[1] // tile):
+        here = slice(n * tile, (n + 1) * tile)
+        there = slice(first + n * tile, first + (n + 1) * tile)
+        acc = jnp.dot(lhs[0], own_w[:, there], preferred_element_type=f32) + jnp.dot(
+            lhs[1], other_w[:, there], preferred_element_type=f32
+        )
+        stay_ref[:, here] = acc[:piece]
+        for g, ref in enumerate(leave_refs):
+            ref[:, here] = acc[(g + 1) * piece : (g + 2) * piece].astype(bf16)
 
 
 def project(own, other, own_w, other_w, slabs, slab, after, beside):
-    parts, (groups, piece, width) = len(own), own[0].shape
-    depth, cols = own_w.shape
-    unit = cols // sum(slabs)
-    tile = math.gcd(cols * slabs[slab] // sum(slabs), 1024)
-    tile = math.gcd(tile, sum(slabs[:slab]) * unit) if slab else tile
-    first, cols = sum(slabs[:slab]) * unit // tile, slabs[slab] * unit
-    lhs = pl.BlockSpec((groups, piece, width), lambda n: (0, 0, 0))
-    weight = pl.BlockSpec((depth, tile), lambda n: (0, first + n))
-    out = pl.BlockSpec((piece, tile), lambda n: (0, n))
-    return pl.pallas_call(
-        ordered(functools.partial(project_kernel, parts), len(after), 0),
-        grid=(cols // tile,),
+    groups, piece, _ = own.shape
+    unit = own_w.shape[1] // sum(slabs)
+    first, cols = sum(slabs[:slab]) * unit, slabs[slab] * unit
+    return pl.pallas_call(
+        ordered(
+            functools.partial(project_kernel, first, math.gcd(unit, 512)), len(after), 0
+        ),
         out_shape=[jax.ShapeDtypeStruct((piece, cols), f32)]
         + [jax.ShapeDtypeStruct((piece, cols), bf16)] * (groups - 1),
-        in_specs=waits(after) + [lhs] * (2 * parts) + [weight, weight],
-        out_specs=[out] * groups,
+        in_specs=waits(after) + vmem(4),
+        out_specs=vmem(groups),
         compiler_params=params(),
         cost_estimate=busy(beside),
         name="project",
-    )(*after, *own, *other, own_w, other_w)
+    )(*after, own, other, own_w, other_w)
 
 
 def finish_kernel(counts, *refs):
@@ -590,7 +582,7 @@
         stay, leave = attend_prior(
             where, locals_[n], ends[n], piece, dh, last, 1 if n + 1 < seqs else 0
         )
-        own[n], other[n] = [stay], [swap(leave, "head", 1)]
+        own[n], other[n] = stay, swap(leave, "head", 1)
         last[:] = [stay]
 
     def multiply(s, slab):

time: 113 us -> 112 us (level)
  Pallas kernels: 38.9 us -> 35.4 us
  waiting for transfers between devices: 33.3 us -> 36 us
    pallas_call x4, Pallas kernels: 11 us -> 7.32 us  [project(): pl.pallas_call(ordered(functools.partial(project_kernel, first, math.gcd(...]
    ppermute x27, waiting for transfers between devices: 33.3 us -> 36 us  [swap(): lax.ppermute(value, axis, [(j, j ^ bit) for j in range(lax.axis_size(axis...]
  transfers between devices with their start and end apart: 27 -> 27, of which waited for: 13 -> 14; matrix products, arithmetic and copies ran while one was open for 7% -> 7% of each run, Pallas kernels for 28% -> 25%
where the time goes in v1:
time: 112 us
  waiting for transfers between devices  36 us (32%)
  Pallas kernels  35.4 us (32%)
  starting transfers between devices  31 us (28%)
  local copies, waits for them, and re-layouts  8.75 us (8%)
    ppermute x27, waiting for transfers between devices, swap(): lax.ppermute(value, axis, [(j, j ^ bit) for j in range(lax.axis_size(axis...  36 us
    ppermute x27, starting transfers between devices, swap(): lax.ppermute(value, axis, [(j, j ^ bit) for j in range(lax.axis_size(axis...  31 us
    unnamed x20, local copies, waits for them, and re-layouts  8.75 us
    pallas_call x3, Pallas kernels, attend_local(): pl.pallas_call(ordered(functools.partial(local_kernel, first, q_at, v_at,...  8.64 us
    pallas_call x4, Pallas kernels, project(): pl.pallas_call(ordered(functools.partial(project_kernel, first, math.gcd(...  7.32 us
    pallas_call x2, Pallas kernels, pack(): pl.pallas_call(functools.partial(pack_kernel, places, len(arrays)), out_s...  5.62 us
    pallas_call x2, Pallas kernels, block_state(): pl.pallas_call(ordered(functools.partial(state_kernel, k_at, v_at, heads,...  3.88 us
    pallas_call x4, Pallas kernels, chain_step(): pl.pallas_call(ordered(functools.partial(step_kernel, levels), len(after)...  2.88 us
  transfers between devices with their start and end apart: 27, of which 14 were waited for; matrix products, arithmetic and copies ran while one was open for 7% of the time, Pallas kernels for 25%

profile of v1, /device:TPU:0, one launch (start us, length us, event | category | flops | bytes accessed | tf_op | source)
XLA Modules:
  0.0 112.1 jit_solution(5266172988653849259)
XLA Ops:
  0.6 4.1 %pack.2 = (bf16[1,2,96,1024]{3,2,1,0:T(8,128)(2,1)}, bf16[1,2,96,1024]{3,2,1,0:T(8,128)(2,1)}, bf16[1,10,96,1024]{3,2,1,0:T(8,128)(2,1)}) custom-call(s32[3]{0:T(128)} %pad_add_fusion.where_ref.refs_1_, bf16[2,3,96,4096]{3,2,1,0:T(8,128)(2,1)} %bitcast.8), custom_call_target="tpu_custom_call" | custom-call | tf_op jit(solution)/shard_map/pack/pallas_call | solution.py:135
  5.2 2.6 %collective-permute-start.1 = (bf16[1,2,96,1024]{3,2,1,0:T(8,128)(2,1)}, bf16[1,2,96,1024]{3,2,1,0:T(8,128)(2,1)}, u32[]{:S(2)}, u32[]{:S(2)}) collective-permute-start(bf16[1,2,96,1024]{3,2,1,0:T(8,128)(2,1)} %get-tuple-element.55), channel_id=1, source_target_pairs={{0,2},{1,3},{2,0},{3,1},{4,6},{5,7},{6,4},{7,5},{8,10},{9,11},{10,... | collective-permute-start | bytes 1179656 | tf_op jit(solution)/shard_map/ppermute | solution.py:47
  7.9 7.9 %copy.8.refs_0_ = bf16[1024,4096]{1,0:T(8,128)(2,1)} copy(bf16[1024,4096]{1,0:T(8,128)(2,1)} %refs_3_.5) | data formatting | bytes 16777216
  19.7 6.3 %collective-permute-done.2.refs_4_.refs_6_.refs_10_ = bf16[1,2,96,1024]{3,2,1,0:T(8,128)(2,1)} collective-permute-done((bf16[1,2,96,1024]{3,2,1,0:T(8,128)(2,1)}, bf16[1,2,96,1024]{3,2,1,0:T(8,128)(2,1)}, u32[]{:S(2)}, u32[]{:S(2)}) %collective-permute-start.2) | collective-permute-done | bytes 393248 | tf_op jit(solution)/shard_map/ppermute | solution.py:47
  26.0 2.4 %block_state.2 = (bf16[8,192,256]{2,1,0:T(8,128)(2,1)S(1)}, f32[272,256]{1,0:T(8,128)S(1)}, bf16[272,256]{1,0:T(8,128)(2,1)S(1)}, bf16[272,256]{1,0:T(8,128)(2,1)S(1)}, bf16[272,256]{1,0:T(8,128)(2,1)S(1)}) custom-call(bf16[8,192,256]{2,1,0:T(8,128)(2,1)S(1)} %get-tuple-element.54.refs_0_.refs_3_, s32[3]{0:T(128)S(1)} %copy-done, ...), custom_call_target="tpu_custom_call" | custom-call | tf_op jit(solution)/shard_map/block_state/pallas_call | solution.py:227
  28.5 1.7 %collective-permute-start.7 = (bf16[2,2,96,1024]{3,2,1,0:T(8,128)(2,1)S(1)}, bf16[2,2,96,1024]{3,2,1,0:T(8,128)(2,1)S(1)}, u32[]{:S(2)}, u32[]{:S(2)}) collective-permute-start(bf16[2,2,96,1024]{3,2,1,0:T(8,128)(2,1)S(1)} %get-tuple-element.66), channel_id=1, source_target_pairs={{0,2},{1,3},{2,0},{3,1},{4,6},{5,7},{6,4},{7,5},{8,10},{9,11},{10,... | collective-permute-start | bytes 2359304 | tf_op jit(solution)/shard_map/ppermute | solution.py:47
  36.3 2.1 %collective-permute-done.4.refs_4_ = bf16[272,256]{1,0:T(8,128)(2,1)S(1)} collective-permute-done((bf16[272,256]{1,0:T(8,128)(2,1)S(1)}, bf16[272,256]{1,0:T(8,128)(2,1)S(1)}, u32[]{:S(2)}, u32[]{:S(2)}) %collective-permute-start.4) | collective-permute-done | bytes 139296 | tf_op jit(solution)/shard_map/ppermute | solution.py:47
  38.3 1.6 %collective-permute-done.5.refs_5_ = bf16[272,256]{1,0:T(8,128)(2,1)S(1)} collective-permute-done((bf16[272,256]{1,0:T(8,128)(2,1)S(1)}, bf16[272,256]{1,0:T(8,128)(2,1)S(1)}, u32[]{:S(2)}, u32[]{:S(2)}) %collective-permute-start.5) | collective-permute-done | bytes 139296 | tf_op jit(solution)/shard_map/ppermute | solution.py:47
  40.6 2.7 %collective-permute-start.6 = (bf16[272,256]{1,0:T(8,128)(2,1)S(1)}, bf16[272,256]{1,0:T(8,128)(2,1)S(1)}, u32[]{:S(2)}, u32[]{:S(2)}) collective-permute-start(bf16[272,256]{1,0:T(8,128)(2,1)S(1)} %chain_step.4.refs_0_), channel_id=1, source_target_pairs={{0,16},{4,20},{8,24},{12,28},{16,0},{20,4},{24,8},{28,12},{1,17},{... | collective-permute-start | bytes 417800 | tf_op jit(solution)/shard_map/ppermute | solution.py:47
  43.2 2.6 %attend_local.3 = (bf16[8,192,256]{2,1,0:T(8,128)(2,1)S(1)}, f32[8,192,256]{2,1,0:T(8,128)S(1)}) custom-call(bf16[272,256]{1,0:T(8,128)(2,1)S(1)} %chain_step.4.refs_0_, s32[3]{0:T(128)S(1)} %copy-done, bf16[8,256,256]{2,1,0:T(8,128)(2,1)S(1)} %integer_maps.1.refs_1_.refs_2_, bf16[8,192,256]{2,1,0:T(8,128)(2,1)S(1)} %get-tuple-element.54.refs_0_.refs_3_, ...), custom_call_target="tpu_custom_call" | custom-call | flops 3000000000 | tf_op jit(solution)/shard_map/attend_local/pallas_call | solution.py:320
  45.9 3.5 %collective-permute-done.6.refs_6_ = bf16[272,256]{1,0:T(8,128)(2,1)S(1)} collective-permute-done((bf16[272,256]{1,0:T(8,128)(2,1)S(1)}, bf16[272,256]{1,0:T(8,128)(2,1)S(1)}, u32[]{:S(2)}, u32[]{:S(2)}) %collective-permute-start.6) | collective-permute-done | bytes 139296 | tf_op jit(solution)/shard_map/ppermute | solution.py:47
  50.6 2.2 %collective-permute-start.11 = (bf16[272,256]{1,0:T(8,128)(2,1)S(1)}, bf16[272,256]{1,0:T(8,128)(2,1)S(1)}, u32[]{:S(2)}, u32[]{:S(2)}) collective-permute-start(bf16[272,256]{1,0:T(8,128)(2,1)S(1)} %get-tuple-element.75), channel_id=1, source_target_pairs={{0,12},{4,8},{8,4},{12,0},{16,28},{20,24},{24,20},{28,16},{1,13},{... | collective-permute-start | bytes 417800 | tf_op jit(solution)/shard_map/ppermute | solution.py:47
  60.3 2.6 %attend_local.4 = (bf16[8,192,256]{2,1,0:T(8,128)(2,1)S(1)}, f32[8,192,256]{2,1,0:T(8,128)S(1)}) custom-call(f32[272,256]{1,0:T(8,128)S(1)} %get-tuple-element.68.refs_0_.refs_2_, s32[3]{0:T(128)S(1)} %copy-done, bf16[8,256,256]{2,1,0:T(8,128)(2,1)S(1)} %integer_maps.1.refs_1_.refs_2_, bf16[8,192,256]{2,1,0:T(8,128)(2,1)S(1)} %get-tuple-element.54.refs_0_.refs_3_, ...), custom_call_target="tpu_custom_call" | custom-call | flops 3000000000 | tf_op jit(solution)/shard_map/attend_local/pallas_call | solution.py:320
  64.5 1.6 %collective-permute-start.19 = (bf16[2,1,96,1024]{3,2,1,0:T(8,128)(2,1)S(1)}, bf16[2,1,96,1024]{3,2,1,0:T(8,128)(2,1)S(1)}, u32[]{:S(2)}, u32[]{:S(2)}) collective-permute-start(bf16[2,1,96,1024]{3,2,1,0:T(8,128)(2,1)S(1)} %get-tuple-element.85), channel_id=1, source_target_pairs={{0,2},{1,3},{2,0},{3,1},{4,6},{5,7},{6,4},{7,5},{8,10},{9,11},{10,... | collective-permute-start | bytes 1179656 | tf_op jit(solution)/shard_map/ppermute | solution.py:47
  66.9 2.7 %collective-permute-start.18 = (bf16[272,256]{1,0:T(8,128)(2,1)S(1)}, bf16[272,256]{1,0:T(8,128)(2,1)S(1)}, u32[]{:S(2)}, u32[]{:S(2)}) collective-permute-start(bf16[272,256]{1,0:T(8,128)(2,1)S(1)} %chain_step.6.refs_0_), channel_id=1, source_target_pairs={{0,16},{4,20},{8,24},{12,28},{16,0},{20,4},{24,8},{28,12},{1,17},{... | collective-permute-start | bytes 417800 | tf_op jit(solution)/shard_map/ppermute | solution.py:47
  69.7 3.5 %project.4 = (f32[96,4096]{1,0:T(8,128)S(1)}, bf16[96,4096]{1,0:T(8,128)(2,1)S(1)}) custom-call(bf16[272,256]{1,0:T(8,128)(2,1)S(1)} %chain_step.6.refs_0_, bf16[2,96,1024]{2,1,0:T(8,128)(2,1)S(1)} %get-tuple-element.76.refs_0_.refs_1_, bf16[2,96,1024]{2,1,0:T(8,128)(2,1)S(1)} %collective-permute-done.15.refs_2_, bf16[1024,4096]{1,0:T(8,128)(2,1)S(1)} %bitcast.5, ...), custom_call_target="tpu_custom_call" | custom-call | flops 6000000000 | tf_op jit(solution)/shard_map/project/pallas_call | solution.py:401
  74.7 1.7 %collective-permute-done.18.refs_6_ = bf16[272,256]{1,0:T(8,128)(2,1)S(1)} collective-permute-done((bf16[272,256]{1,0:T(8,128)(2,1)S(1)}, bf16[272,256]{1,0:T(8,128)(2,1)S(1)}, u32[]{:S(2)}, u32[]{:S(2)}) %collective-permute-start.18) | collective-permute-done | bytes 139296 | tf_op jit(solution)/shard_map/ppermute | solution.py:47
  80.8 3.4 %attend_local.5 = (bf16[8,384,256]{2,1,0:T(8,128)(2,1)S(1)}, f32[8,384,256]{2,1,0:T(8,128)S(1)}) custom-call(bf16[272,256]{1,0:T(8,128)(2,1)S(1)} %get-tuple-element.83.refs_0_.refs_4_, s32[3]{0:T(128)S(1)} %copy-done, bf16[8,256,256]{2,1,0:T(8,128)(2,1)S(1)} %integer_maps.1.refs_1_.refs_2_, bf16[8,192,256]{2,1,0:T(8,128)(2,1)S(1)} %get-tuple-element.59.refs_0_.refs_3_, ...), custom_call_target="tpu_custom_call" | custom-call | flops 3000000000 | tf_op jit(solution)/shard_map/attend_local/pallas_call | solution.py:320
  85.0 1.9 %collective-permute-done.22.refs_7_ = bf16[272,256]{1,0:T(8,128)(2,1)S(1)} collective-permute-done((bf16[272,256]{1,0:T(8,128)(2,1)S(1)}, bf16[272,256]{1,0:T(8,128)(2,1)S(1)}, u32[]{:S(2)}, u32[]{:S(2)}) %collective-permute-start.22) | collective-permute-done | bytes 139296 | tf_op jit(solution)/shard_map/ppermute | solution.py:47
  88.1 1.7 %collective-permute-done.23.refs_2_.refs_3_ = bf16[2,96,1024]{2,1,0:T(8,128)(2,1)S(1)} collective-permute-done((bf16[2,96,1024]{2,1,0:T(8,128)(2,1)S(1)}, bf16[2,96,1024]{2,1,0:T(8,128)(2,1)S(1)}, u32[]{:S(2)}, u32[]{:S(2)}) %collective-permute-start.23) | collective-permute-done | bytes 393248 | tf_op jit(solution)/shard_map/ppermute | solution.py:47
  89.8 1.8 %project.5 = (f32[96,2048]{1,0:T(8,128)S(1)}, bf16[96,2048]{1,0:T(8,128)(2,1)S(1)}) custom-call(bf16[2,96,1024]{2,1,0:T(8,128)(2,1)S(1)} %get-tuple-element.91.refs_0_.refs_1_.refs_2_, bf16[2,96,1024]{2,1,0:T(8,128)(2,1)S(1)} %get-tuple-element.91.refs_0_.refs_1_.refs_2_, bf16[2,96,1024]{2,1,0:T(8,128)(2,1)S(1)} %collective-permute-done.23.refs_2_.refs_3_, ...), custom_call_target="tpu_custom_call" | custom-call | tf_op jit(solution)/shard_map/project/pallas_call | solution.py:401
  94.3 1.6 %collective-permute-start.25 = (bf16[96,1536]{1,0:T(8,128)(2,1)S(1)}, bf16[96,1536]{1,0:T(8,128)(2,1)S(1)}, u32[]{:S(2)}, u32[]{:S(2)}) collective-permute-start(bf16[96,1536]{1,0:T(8,128)(2,1)S(1)} %get-tuple-element.96), channel_id=1, source_target_pairs={{0,2},{1,3},{2,0},{3,1},{4,6},{5,7},{6,4},{7,5},{8,10},{9,11},{10,... | collective-permute-start | bytes 884744 | tf_op jit(solution)/shard_map/ppermute | solution.py:47
  97.1 6.6 %collective-permute-done.24.refs_3_ = bf16[96,2048]{1,0:T(8,128)(2,1)S(1)} collective-permute-done((bf16[96,2048]{1,0:T(8,128)(2,1)S(1)}, bf16[96,2048]{1,0:T(8,128)(2,1)S(1)}, u32[]{:S(2)}, u32[]{:S(2)}) %collective-permute-start.24) | collective-permute-done | bytes 393248 | tf_op jit(solution)/shard_map/ppermute | solution.py:47
  103.7 6.3 %collective-permute-done.25.refs_5_ = bf16[96,1536]{1,0:T(8,128)(2,1)S(1)} collective-permute-done((bf16[96,1536]{1,0:T(8,128)(2,1)S(1)}, bf16[96,1536]{1,0:T(8,128)(2,1)S(1)}, u32[]{:S(2)}, u32[]{:S(2)}) %collective-permute-start.25) | collective-permute-done | bytes 294944 | tf_op jit(solution)/shard_map/ppermute | solution.py:47
  (77 shorter events, 36.5 us)
Async XLA Ops:
  4.7 12.5 %collective-permute-start = (bf16[1,10,96,1024]{3,2,1,0:T(8,128)(2,1)}, bf16[1,10,96,1024]{3,2,1,0:T(8,128)(2,1)S(1)}, u32[]{:S(2)}, u32[]{:S(2)}) collective-permute-start(bf16[1,10,96,1024]{3,2,1,0:T(8,128)(2,1)} %get-tuple-element.52), channel_id=1, source_target_pairs={{0,1},{1,0},{2,3},{3,2},{4,5},{5,4},{6,7},{7,6},{8,9},{9,8},{10,11... | collective-permute-start | bytes 5898248 | tf_op jit(solution)/shard_map/ppermute | solution.py:47
  5.2 14.5 %collective-permute-start.1 = (bf16[1,2,96,1024]{3,2,1,0:T(8,128)(2,1)}, bf16[1,2,96,1024]{3,2,1,0:T(8,128)(2,1)}, u32[]{:S(2)}, u32[]{:S(2)}) collective-permute-start(bf16[1,2,96,1024]{3,2,1,0:T(8,128)(2,1)} %get-tuple-element.55), channel_id=1, source_target_pairs={{0,2},{1,3},{2,0},{3,1},{4,6},{5,7},{6,4},{7,5},{8,10},{9,11},{10,... | collective-permute-start | bytes 1179656 | tf_op jit(solution)/shard_map/ppermute | solution.py:47
  7.8 18.2 %collective-permute-start.2 = (bf16[1,2,96,1024]{3,2,1,0:T(8,128)(2,1)}, bf16[1,2,96,1024]{3,2,1,0:T(8,128)(2,1)}, u32[]{:S(2)}, u32[]{:S(2)}) collective-permute-start(bf16[1,2,96,1024]{3,2,1,0:T(8,128)(2,1)} %get-tuple-element.56), channel_id=1, source_target_pairs={{0,3},{1,2},{2,1},{3,0},{4,7},{5,6},{6,5},{7,4},{8,11},{9,10},{10,... | collective-permute-start | bytes 1179656 | tf_op jit(solution)/shard_map/ppermute | solution.py:47
  28.4 41.3 %collective-permute-start.16 = (bf16[1024,4096]{1,0:T(8,128)(2,1)S(1)}, bf16[1024,4096]{1,0:T(8,128)(2,1)S(1)}, u32[]{:S(2)}, u32[]{:S(2)}) collective-permute-start(bf16[1024,4096]{1,0:T(8,128)(2,1)S(1)} %later_than.1), channel_id=1, source_target_pairs={{0,1},{1,0},{2,3},{3,2},{4,5},{5,4},{6,7},{7,6},{8,9},{9,8},{10,11... | collective-permute-start | bytes 25165832 | tf_op jit(solution)/shard_map/ppermute | solution.py:47
  28.5 24.2 %collective-permute-start.7 = (bf16[2,2,96,1024]{3,2,1,0:T(8,128)(2,1)S(1)}, bf16[2,2,96,1024]{3,2,1,0:T(8,128)(2,1)S(1)}, u32[]{:S(2)}, u32[]{:S(2)}) collective-permute-start(bf16[2,2,96,1024]{3,2,1,0:T(8,128)(2,1)S(1)} %get-tuple-element.66), channel_id=1, source_target_pairs={{0,2},{1,3},{2,0},{3,1},{4,6},{5,7},{6,4},{7,5},{8,10},{9,11},{10,... | collective-permute-start | bytes 2359304 | tf_op jit(solution)/shard_map/ppermute | solution.py:47
  31.8 6.6 %collective-permute-start.4 = (bf16[272,256]{1,0:T(8,128)(2,1)S(1)}, bf16[272,256]{1,0:T(8,128)(2,1)S(1)}, u32[]{:S(2)}, u32[]{:S(2)}) collective-permute-start(bf16[272,256]{1,0:T(8,128)(2,1)S(1)} %get-tuple-element.61), channel_id=1, source_target_pairs={{0,8},{4,12},{8,0},{12,4},{16,24},{20,28},{24,16},{28,20},{1,9},{5... | collective-permute-start | bytes 417800 | tf_op jit(solution)/shard_map/ppermute | solution.py:47
  33.3 6.6 %collective-permute-start.5 = (bf16[272,256]{1,0:T(8,128)(2,1)S(1)}, bf16[272,256]{1,0:T(8,128)(2,1)S(1)}, u32[]{:S(2)}, u32[]{:S(2)}) collective-permute-start(bf16[272,256]{1,0:T(8,128)(2,1)S(1)} %get-tuple-element.62), channel_id=1, source_target_pairs={{0,12},{4,8},{8,4},{12,0},{16,28},{20,24},{24,20},{28,16},{1,13},{... | collective-permute-start | bytes 417800 | tf_op jit(solution)/shard_map/ppermute | solution.py:47
  35.8 21.0 %collective-permute-start.8 = (bf16[2,1,96,1024]{3,2,1,0:T(8,128)(2,1)S(1)}, bf16[2,1,96,1024]{3,2,1,0:T(8,128)(2,1)S(1)}, u32[]{:S(2)}, u32[]{:S(2)}) collective-permute-start(bf16[2,1,96,1024]{3,2,1,0:T(8,128)(2,1)S(1)} %get-tuple-element.69), channel_id=1, source_target_pairs={{0,2},{1,3},{2,0},{3,1},{4,6},{5,7},{6,4},{7,5},{8,10},{9,11},{10,... | collective-permute-start | bytes 1179656 | tf_op jit(solution)/shard_map/ppermute | solution.py:47
  40.6 8.8 %collective-permute-start.6 = (bf16[272,256]{1,0:T(8,128)(2,1)S(1)}, bf16[272,256]{1,0:T(8,128)(2,1)S(1)}, u32[]{:S(2)}, u32[]{:S(2)}) collective-permute-start(bf16[272,256]{1,0:T(8,128)(2,1)S(1)} %chain_step.4.refs_0_), channel_id=1, source_target_pairs={{0,16},{4,20},{8,24},{12,28},{16,0},{20,4},{24,8},{28,12},{1,17},{... | collective-permute-start | bytes 417800 | tf_op jit(solution)/shard_map/ppermute | solution.py:47
  50.2 8.2 %collective-permute-start.10 = (bf16[272,256]{1,0:T(8,128)(2,1)S(1)}, bf16[272,256]{1,0:T(8,128)(2,1)S(1)}, u32[]{:S(2)}, u32[]{:S(2)}) collective-permute-start(bf16[272,256]{1,0:T(8,128)(2,1)S(1)} %get-tuple-element.74), channel_id=1, source_target_pairs={{0,8},{4,12},{8,0},{12,4},{16,24},{20,28},{24,16},{28,20},{1,9},{5... | collective-permute-start | bytes 417800 | tf_op jit(solution)/shard_map/ppermute | solution.py:47
  50.6 9.4 %collective-permute-start.11 = (bf16[272,256]{1,0:T(8,128)(2,1)S(1)}, bf16[272,256]{1,0:T(8,128)(2,1)S(1)}, u32[]{:S(2)}, u32[]{:S(2)}) collective-permute-start(bf16[272,256]{1,0:T(8,128)(2,1)S(1)} %get-tuple-element.75), channel_id=1, source_target_pairs={{0,12},{4,8},{8,4},{12,0},{16,28},{20,24},{24,20},{28,16},{1,13},{... | collective-permute-start | bytes 417800 | tf_op jit(solution)/shard_map/ppermute | solution.py:47
  52.8 10.2 %collective-permute-start.9 = (bf16[272,256]{1,0:T(8,128)(2,1)S(1)}, bf16[272,256]{1,0:T(8,128)(2,1)S(1)}, u32[]{:S(2)}, u32[]{:S(2)}) collective-permute-start(bf16[272,256]{1,0:T(8,128)(2,1)S(1)} %get-tuple-element.73), channel_id=1, source_target_pairs={{0,4},{4,0},{8,12},{12,8},{16,20},{20,16},{24,28},{28,24},{1,5},{5... | collective-permute-start | bytes 417800 | tf_op jit(solution)/shard_map/ppermute | solution.py:47
  56.8 7.7 %collective-permute-start.12 = (bf16[272,256]{1,0:T(8,128)(2,1)S(1)}, bf16[272,256]{1,0:T(8,128)(2,1)S(1)}, u32[]{:S(2)}, u32[]{:S(2)}) collective-permute-start(bf16[272,256]{1,0:T(8,128)(2,1)S(1)} %get-tuple-element.77), channel_id=1, source_target_pairs={{0,4},{4,0},{8,12},{12,8},{16,20},{20,16},{24,28},{28,24},{1,5},{5... | collective-permute-start | bytes 417800 | tf_op jit(solution)/shard_map/ppermute | solution.py:47
  58.4 7.8 %collective-permute-start.13 = (bf16[272,256]{1,0:T(8,128)(2,1)S(1)}, bf16[272,256]{1,0:T(8,128)(2,1)S(1)}, u32[]{:S(2)}, u32[]{:S(2)}) collective-permute-start(bf16[272,256]{1,0:T(8,128)(2,1)S(1)} %get-tuple-element.78), channel_id=1, source_target_pairs={{0,8},{4,12},{8,0},{12,4},{16,24},{20,28},{24,16},{28,20},{1,9},{5... | collective-permute-start | bytes 417800 | tf_op jit(solution)/shard_map/ppermute | solution.py:47
  59.9 6.4 %collective-permute-start.14 = (bf16[272,256]{1,0:T(8,128)(2,1)S(1)}, bf16[272,256]{1,0:T(8,128)(2,1)S(1)}, u32[]{:S(2)}, u32[]{:S(2)}) collective-permute-start(bf16[272,256]{1,0:T(8,128)(2,1)S(1)} %get-tuple-element.79), channel_id=1, source_target_pairs={{0,12},{4,8},{8,4},{12,0},{16,28},{20,24},{24,20},{28,16},{1,13},{... | collective-permute-start | bytes 417800 | tf_op jit(solution)/shard_map/ppermute | solution.py:47
  64.5 16.3 %collective-permute-start.19 = (bf16[2,1,96,1024]{3,2,1,0:T(8,128)(2,1)S(1)}, bf16[2,1,96,1024]{3,2,1,0:T(8,128)(2,1)S(1)}, u32[]{:S(2)}, u32[]{:S(2)}) collective-permute-start(bf16[2,1,96,1024]{3,2,1,0:T(8,128)(2,1)S(1)} %get-tuple-element.85), channel_id=1, source_target_pairs={{0,2},{1,3},{2,0},{3,1},{4,6},{5,7},{6,4},{7,5},{8,10},{9,11},{10,... | collective-permute-start | bytes 1179656 | tf_op jit(solution)/shard_map/ppermute | solution.py:47
  66.9 9.5 %collective-permute-start.18 = (bf16[272,256]{1,0:T(8,128)(2,1)S(1)}, bf16[272,256]{1,0:T(8,128)(2,1)S(1)}, u32[]{:S(2)}, u32[]{:S(2)}) collective-permute-start(bf16[272,256]{1,0:T(8,128)(2,1)S(1)} %chain_step.6.refs_0_), channel_id=1, source_target_pairs={{0,16},{4,20},{8,24},{12,28},{16,0},{20,4},{24,8},{28,12},{1,17},{... | collective-permute-start | bytes 417800 | tf_op jit(solution)/shard_map/ppermute | solution.py:47
  73.2 19.7 %collective-permute-start.17 = (bf16[96,4096]{1,0:T(8,128)(2,1)S(1)}, bf16[96,4096]{1,0:T(8,128)(2,1)S(1)}, u32[]{:S(2)}, u32[]{:S(2)}) collective-permute-start(bf16[96,4096]{1,0:T(8,128)(2,1)S(1)} %get-tuple-element.82), channel_id=1, source_target_pairs={{0,2},{1,3},{2,0},{3,1},{4,6},{5,7},{6,4},{7,5},{8,10},{9,11},{10,... | collective-permute-start | bytes 2359304 | tf_op jit(solution)/shard_map/ppermute | solution.py:47
  77.3 6.9 %collective-permute-start.20 = (bf16[272,256]{1,0:T(8,128)(2,1)S(1)}, bf16[272,256]{1,0:T(8,128)(2,1)S(1)}, u32[]{:S(2)}, u32[]{:S(2)}) collective-permute-start(bf16[272,256]{1,0:T(8,128)(2,1)S(1)} %get-tuple-element.88), channel_id=1, source_target_pairs={{0,4},{4,0},{8,12},{12,8},{16,20},{20,16},{24,28},{28,24},{1,5},{5... | collective-permute-start | bytes 417800 | tf_op jit(solution)/shard_map/ppermute | solution.py:47
  78.8 6.1 %collective-permute-start.21 = (bf16[272,256]{1,0:T(8,128)(2,1)S(1)}, bf16[272,256]{1,0:T(8,128)(2,1)S(1)}, u32[]{:S(2)}, u32[]{:S(2)}) collective-permute-start(bf16[272,256]{1,0:T(8,128)(2,1)S(1)} %get-tuple-element.89), channel_id=1, source_target_pairs={{0,8},{4,12},{8,0},{12,4},{16,24},{20,28},{24,16},{28,20},{1,9},{5... | collective-permute-start | bytes 417800 | tf_op jit(solution)/shard_map/ppermute | solution.py:47
  79.5 7.3 %collective-permute-start.22 = (bf16[272,256]{1,0:T(8,128)(2,1)S(1)}, bf16[272,256]{1,0:T(8,128)(2,1)S(1)}, u32[]{:S(2)}, u32[]{:S(2)}) collective-permute-start(bf16[272,256]{1,0:T(8,128)(2,1)S(1)} %get-tuple-element.90), channel_id=1, source_target_pairs={{0,12},{4,8},{8,4},{12,0},{16,28},{20,24},{24,20},{28,16},{1,13},{... | collective-permute-start | bytes 417800 | tf_op jit(solution)/shard_map/ppermute | solution.py:47
  91.7 12.0 %collective-permute-start.24 = (bf16[96,2048]{1,0:T(8,128)(2,1)S(1)}, bf16[96,2048]{1,0:T(8,128)(2,1)S(1)}, u32[]{:S(2)}, u32[]{:S(2)}) collective-permute-start(bf16[96,2048]{1,0:T(8,128)(2,1)S(1)} %get-tuple-element.94), channel_id=1, source_target_pairs={{0,2},{1,3},{2,0},{3,1},{4,6},{5,7},{6,4},{7,5},{8,10},{9,11},{10,... | collective-permute-start | bytes 1179656 | tf_op jit(solution)/shard_map/ppermute | solution.py:47
  94.3 15.7 %collective-permute-start.25 = (bf16[96,1536]{1,0:T(8,128)(2,1)S(1)}, bf16[96,1536]{1,0:T(8,128)(2,1)S(1)}, u32[]{:S(2)}, u32[]{:S(2)}) collective-permute-start(bf16[96,1536]{1,0:T(8,128)(2,1)S(1)} %get-tuple-element.96), channel_id=1, source_target_pairs={{0,2},{1,3},{2,0},{3,1},{4,6},{5,7},{6,4},{7,5},{8,10},{9,11},{10,... | collective-permute-start | bytes 884744 | tf_op jit(solution)/shard_map/ppermute | solution.py:47
  96.5 14.9 %collective-permute-start.26 = (bf16[96,512]{1,0:T(8,128)(2,1)S(1)}, bf16[96,512]{1,0:T(8,128)(2,1)S(1)}, u32[]{:S(2)}, u32[]{:S(2)}) collective-permute-start(bf16[96,512]{1,0:T(8,128)(2,1)S(1)} %get-tuple-element.98), channel_id=1, source_target_pairs={{0,2},{1,3},{2,0},{3,1},{4,6},{5,7},{6,4},{7,5},{8,10},{9,11},{10,... | collective-permute-start | bytes 294920 | tf_op jit(solution)/shard_map/ppermute | solution.py:47
  (12 other events, 79.3 us)

commit v2 on v1

--- a/solution.py
+++ b/solution.py
@@ -380,36 +380,67 @@
     )(*after, where, *values, *shares)
 
 
-def project_kernel(first, tile, own_ref, other_ref, own_w, other_w, stay_ref, *leave_refs):
-    groups, piece, width = own_ref.shape
-    lhs = [ref[...].reshape(groups * piece, width) for ref in (own_ref, other_ref)]
-    for n in range(stay_ref.shape[1] // tile):
+def project_kernel(first, tile, begun, lhs_refs, w_refs, *out_refs):
+    groups, piece, width = lhs_refs[0].shape
+    lhs = [ref[...].reshape(groups * piece, width) for ref in lhs_refs]
+    for n in range(out_refs[0].shape[1] // tile):
         here = slice(n * tile, (n + 1) * tile)
         there = slice(first + n * tile, first + (n + 1) * tile)
-        acc = jnp.dot(lhs[0], own_w[:, there], preferred_element_type=f32) + jnp.dot(
-            lhs[1], other_w[:, there], preferred_element_type=f32
-        )
-        stay_ref[:, here] = acc[:piece]
-        for g, ref in enumerate(leave_refs):
-            ref[:, here] = acc[(g + 1) * piece : (g + 2) * piece].astype(bf16)
-
-
-def project(own, other, own_w, other_w, slabs, slab, after, beside):
+        acc = None if begun is None else begun[:, here]
+        for value, w_ref in zip(lhs, w_refs):
+            term = jnp.dot(value, w_ref[:, there], preferred_element_type=f32)
+            acc = term if acc is None else acc + term
+        if len(out_refs) == 1:
+            out_refs[0][:, here] = acc
+        else:
+            for g, ref in enumerate(out_refs):
+                ref[:, here] = acc[g * piece : (g + 1) * piece].astype(ref.dtype)
+
+
+def begin_kernel(first, tile, lhs_ref, w_ref, out_ref):
+    project_kernel(first, tile, None, [lhs_ref], [w_ref], out_ref)
+
+
+def whole_kernel(first, tile, own_ref, other_ref, own_w, other_w, *out_refs):
+    project_kernel(first, tile, None, [own_ref, other_ref], [own_w, other_w], *out_refs)
+
+
+def end_kernel(first, tile, begun_ref, other_ref, other_w, *out_refs):
+    project_kernel(first, tile, begun_ref, [other_ref], [other_w], *out_refs)
+
+
+def begin_project(own, own_w, slabs, slab, after):
     groups, piece, _ = own.shape
     unit = own_w.shape[1] // sum(slabs)
     first, cols = sum(slabs[:slab]) * unit, slabs[slab] * unit
     return pl.pallas_call(
-        ordered(
-            functools.partial(project_kernel, first, math.gcd(unit, 512)), len(after), 0
-        ),
+        ordered(functools.partial(begin_kernel, first, math.gcd(unit, 512)), len(after), 0),
+        out_shape=jax.ShapeDtypeStruct((groups * piece, cols), f32),
+        in_specs=waits(after) + vmem(2),
+        out_specs=vmem(1)[0],
+        compiler_params=params(),
+        cost_estimate=busy(3),
+        name="begin_project",
+    )(*after, own, own_w)
+
+
+def project(own, other, own_w, other_w, slabs, slab, after, beside, begun=None):
+    groups, piece, _ = own.shape
+    unit = own_w.shape[1] // sum(slabs)
+    first, cols = sum(slabs[:slab]) * unit, slabs[slab] * unit
+    kernel, values = whole_kernel, (own, other, own_w, other_w)
+    if begun is not None:
+        kernel, values = end_kernel, (begun, other, other_w)
+    return pl.pallas_call(
+        ordered(functools.partial(kernel, first, math.gcd(unit, 512)), len(after), 0),
         out_shape=[jax.ShapeDtypeStruct((piece, cols), f32)]
         + [jax.ShapeDtypeStruct((piece, cols), bf16)] * (groups - 1),
-        in_specs=waits(after) + vmem(4),
+        in_specs=waits(after) + vmem(len(values)),
         out_specs=vmem(groups),
         compiler_params=params(),
         cost_estimate=busy(beside),
         name="project",
-    )(*after, own, other, own_w, other_w)
+    )(*after, *values)
 
 
 def finish_kernel(counts, *refs):
@@ -590,8 +621,12 @@
             for key in totals:
                 if key[0] < s:
                     last.extend(totals[key][1])
+        begun = None
+        if s == seqs - 1 and slab == 0:
+            begun = begin_project(own[s], out_weight, slabs[s], slab, last)
+            last[:] = [begun]
         total, *shares = project(
-            own[s], other[s], out_weight, other_weight, slabs[s], slab, last, 0 if s == seqs - 1 else 6
+            own[s], other[s], out_weight, other_weight, slabs[s], slab, last, 0 if s == seqs - 1 else 6, begun
         )
         totals[s, slab] = total, [swap(v, "head", 2 * (g + 1)) for g, v in enumerate(shares)]
         last[:] = [total]

time: 112 us -> 112 us (level)
  waiting for transfers between devices: 36 us -> 34.1 us
    ppermute x27, waiting for transfers between devices: 36 us -> 34.1 us  [swap(): lax.ppermute(value, axis, [(j, j ^ bit) for j in range(lax.axis_size(axis...]
    pallas_call x4 -> x5, Pallas kernels: 7.32 us -> 7.51 us  [the longest x4 6.52 us: project(): pl.pallas_call(ordered(functools.partial(kernel, first, math.gcd(unit, 51...]
  transfers between devices with their start and end apart: 27 -> 27, of which waited for: 14 -> 14; matrix products, arithmetic and copies ran while one was open for 7% -> 7% of each run, Pallas kernels for 25% -> 26%
where the time goes in v2:
time: 112 us; the launch traced here: 111 us
  Pallas kernels  36.5 us (33%)
  waiting for transfers between devices  34.1 us (30%)
  starting transfers between devices  31.1 us (28%)
  local copies, waits for them, and re-layouts  8.75 us (8%)
    ppermute x27, waiting for transfers between devices, swap(): lax.ppermute(value, axis, [(j, j ^ bit) for j in range(lax.axis_size(axis...  34.1 us
    ppermute x27, starting transfers between devices, swap(): lax.ppermute(value, axis, [(j, j ^ bit) for j in range(lax.axis_size(axis...  31.1 us
    unnamed x20, local copies, waits for them, and re-layouts  8.75 us
    pallas_call x3, Pallas kernels, attend_local(): pl.pallas_call(ordered(functools.partial(local_kernel, first, q_at, v_at,...  8.7 us
    pallas_call x4, Pallas kernels, project(): pl.pallas_call(ordered(functools.partial(kernel, first, math.gcd(unit, 51...  6.52 us
    pallas_call x2, Pallas kernels, pack(): pl.pallas_call(functools.partial(pack_kernel, places, len(arrays)), out_s...  6.39 us
    pallas_call x2, Pallas kernels, block_state(): pl.pallas_call(ordered(functools.partial(state_kernel, k_at, v_at, heads,...  3.91 us
    pallas_call x4, Pallas kernels, chain_step(): pl.pallas_call(ordered(functools.partial(step_kernel, levels), len(after)...  2.92 us
  transfers between devices with their start and end apart: 27, of which 14 were waited for; matrix products, arithmetic and copies ran while one was open for 7% of the time, Pallas kernels for 26%

profile of v2, /device:TPU:0, one launch (start us, length us, event | category | flops | bytes accessed | tf_op | source)
XLA Modules:
  0.0 111.4 jit_solution(15912053700656031006)
XLA Ops:
  0.6 4.1 %pack.2 = (bf16[1,2,96,1024]{3,2,1,0:T(8,128)(2,1)}, bf16[1,2,96,1024]{3,2,1,0:T(8,128)(2,1)}, bf16[1,10,96,1024]{3,2,1,0:T(8,128)(2,1)}) custom-call(s32[3]{0:T(128)} %pad_add_fusion.where_ref.refs_1_, bf16[2,3,96,4096]{3,2,1,0:T(8,128)(2,1)} %bitcast.8), custom_call_target="tpu_custom_call" | custom-call | tf_op jit(solution)/shard_map/pack/pallas_call | solution.py:135
  5.2 2.6 %collective-permute-start.1 = (bf16[1,2,96,1024]{3,2,1,0:T(8,128)(2,1)}, bf16[1,2,96,1024]{3,2,1,0:T(8,128)(2,1)}, u32[]{:S(2)}, u32[]{:S(2)}) collective-permute-start(bf16[1,2,96,1024]{3,2,1,0:T(8,128)(2,1)} %get-tuple-element.55), channel_id=1, source_target_pairs={{0,2},{1,3},{2,0},{3,1},{4,6},{5,7},{6,4},{7,5},{8,10},{9,11},{10,... | collective-permute-start | bytes 1179656 | tf_op jit(solution)/shard_map/ppermute | solution.py:47
  7.9 7.9 %copy.8.refs_0_ = bf16[1024,4096]{1,0:T(8,128)(2,1)} copy(bf16[1024,4096]{1,0:T(8,128)(2,1)} %refs_3_.3) | data formatting | bytes 16777216
  17.2 2.3 %pack.3 = (bf16[2,2,96,1024]{3,2,1,0:T(8,128)(2,1)S(1)}, bf16[2,1,96,1024]{3,2,1,0:T(8,128)(2,1)S(1)}, bf16[2,1,96,1024]{3,2,1,0:T(8,128)(2,1)}, bf16[2,3,96,1024]{3,2,1,0:T(8,128)(2,1)S(1)}) custom-call(s32[3]{0:T(128)S(1)} %copy-done, bf16[2,3,96,4096]{3,2,1,0:T(8,128)(2,1)S(1)} %bitcast.11, ...), custom_call_target="tpu_custom_call" | custom-call | tf_op jit(solution)/shard_map/pack/pallas_call | solution.py:135
  20.4 5.5 %collective-permute-done.2.refs_4_.refs_6_.refs_10_ = bf16[1,2,96,1024]{3,2,1,0:T(8,128)(2,1)} collective-permute-done((bf16[1,2,96,1024]{3,2,1,0:T(8,128)(2,1)}, bf16[1,2,96,1024]{3,2,1,0:T(8,128)(2,1)}, u32[]{:S(2)}, u32[]{:S(2)}) %collective-permute-start.2) | collective-permute-done | bytes 393248 | tf_op jit(solution)/shard_map/ppermute | solution.py:47
  26.0 2.4 %block_state.2 = (bf16[8,192,256]{2,1,0:T(8,128)(2,1)S(1)}, f32[272,256]{1,0:T(8,128)S(1)}, bf16[272,256]{1,0:T(8,128)(2,1)S(1)}, bf16[272,256]{1,0:T(8,128)(2,1)S(1)}, bf16[272,256]{1,0:T(8,128)(2,1)S(1)}) custom-call(bf16[8,192,256]{2,1,0:T(8,128)(2,1)S(1)} %get-tuple-element.54.refs_0_.refs_3_, s32[3]{0:T(128)S(1)} %copy-done, ...), custom_call_target="tpu_custom_call" | custom-call | tf_op jit(solution)/shard_map/block_state/pallas_call | solution.py:227
  28.6 1.7 %collective-permute-start.7 = (bf16[2,2,96,1024]{3,2,1,0:T(8,128)(2,1)S(1)}, bf16[2,2,96,1024]{3,2,1,0:T(8,128)(2,1)S(1)}, u32[]{:S(2)}, u32[]{:S(2)}) collective-permute-start(bf16[2,2,96,1024]{3,2,1,0:T(8,128)(2,1)S(1)} %get-tuple-element.66), channel_id=1, source_target_pairs={{0,2},{1,3},{2,0},{3,1},{4,6},{5,7},{6,4},{7,5},{8,10},{9,11},{10,... | collective-permute-start | bytes 2359304 | tf_op jit(solution)/shard_map/ppermute | solution.py:47
  36.3 2.1 %collective-permute-done.4.refs_4_ = bf16[272,256]{1,0:T(8,128)(2,1)S(1)} collective-permute-done((bf16[272,256]{1,0:T(8,128)(2,1)S(1)}, bf16[272,256]{1,0:T(8,128)(2,1)S(1)}, u32[]{:S(2)}, u32[]{:S(2)}) %collective-permute-start.4) | collective-permute-done | bytes 139296 | tf_op jit(solution)/shard_map/ppermute | solution.py:47
  38.4 1.6 %collective-permute-done.5.refs_5_ = bf16[272,256]{1,0:T(8,128)(2,1)S(1)} collective-permute-done((bf16[272,256]{1,0:T(8,128)(2,1)S(1)}, bf16[272,256]{1,0:T(8,128)(2,1)S(1)}, u32[]{:S(2)}, u32[]{:S(2)}) %collective-permute-start.5) | collective-permute-done | bytes 139296 | tf_op jit(solution)/shard_map/ppermute | solution.py:47
  40.6 2.7 %collective-permute-start.6 = (bf16[272,256]{1,0:T(8,128)(2,1)S(1)}, bf16[272,256]{1,0:T(8,128)(2,1)S(1)}, u32[]{:S(2)}, u32[]{:S(2)}) collective-permute-start(bf16[272,256]{1,0:T(8,128)(2,1)S(1)} %chain_step.4.refs_0_), channel_id=1, source_target_pairs={{0,16},{4,20},{8,24},{12,28},{16,0},{20,4},{24,8},{28,12},{1,17},{... | collective-permute-start | bytes 417800 | tf_op jit(solution)/shard_map/ppermute | solution.py:47
  43.3 2.7 %attend_local.3 = (bf16[8,192,256]{2,1,0:T(8,128)(2,1)S(1)}, f32[8,192,256]{2,1,0:T(8,128)S(1)}) custom-call(bf16[272,256]{1,0:T(8,128)(2,1)S(1)} %chain_step.4.refs_0_, s32[3]{0:T(128)S(1)} %copy-done, bf16[8,256,256]{2,1,0:T(8,128)(2,1)S(1)} %integer_maps.1.refs_1_.refs_2_, bf16[8,192,256]{2,1,0:T(8,128)(2,1)S(1)} %get-tuple-element.54.refs_0_.refs_3_, ...), custom_call_target="tpu_custom_call" | custom-call | flops 3000000000 | tf_op jit(solution)/shard_map/attend_local/pallas_call | solution.py:320
  45.9 3.4 %collective-permute-done.6.refs_6_ = bf16[272,256]{1,0:T(8,128)(2,1)S(1)} collective-permute-done((bf16[272,256]{1,0:T(8,128)(2,1)S(1)}, bf16[272,256]{1,0:T(8,128)(2,1)S(1)}, u32[]{:S(2)}, u32[]{:S(2)}) %collective-permute-start.6) | collective-permute-done | bytes 139296 | tf_op jit(solution)/shard_map/ppermute | solution.py:47
  50.6 2.2 %collective-permute-start.11 = (bf16[272,256]{1,0:T(8,128)(2,1)S(1)}, bf16[272,256]{1,0:T(8,128)(2,1)S(1)}, u32[]{:S(2)}, u32[]{:S(2)}) collective-permute-start(bf16[272,256]{1,0:T(8,128)(2,1)S(1)} %get-tuple-element.75), channel_id=1, source_target_pairs={{0,12},{4,8},{8,4},{12,0},{16,28},{20,24},{24,20},{28,16},{1,13},{... | collective-permute-start | bytes 417800 | tf_op jit(solution)/shard_map/ppermute | solution.py:47
  60.3 2.7 %attend_local.4 = (bf16[8,192,256]{2,1,0:T(8,128)(2,1)S(1)}, f32[8,192,256]{2,1,0:T(8,128)S(1)}) custom-call(f32[272,256]{1,0:T(8,128)S(1)} %get-tuple-element.68.refs_0_.refs_2_, s32[3]{0:T(128)S(1)} %copy-done, bf16[8,256,256]{2,1,0:T(8,128)(2,1)S(1)} %integer_maps.1.refs_1_.refs_2_, bf16[8,192,256]{2,1,0:T(8,128)(2,1)S(1)} %get-tuple-element.54.refs_0_.refs_3_, ...), custom_call_target="tpu_custom_call" | custom-call | flops 3000000000 | tf_op jit(solution)/shard_map/attend_local/pallas_call | solution.py:320
  64.6 1.6 %collective-permute-start.19 = (bf16[2,1,96,1024]{3,2,1,0:T(8,128)(2,1)}, bf16[2,1,96,1024]{3,2,1,0:T(8,128)(2,1)S(1)}, u32[]{:S(2)}, u32[]{:S(2)}) collective-permute-start(bf16[2,1,96,1024]{3,2,1,0:T(8,128)(2,1)} %get-tuple-element.85), channel_id=1, source_target_pairs={{0,2},{1,3},{2,0},{3,1},{4,6},{5,7},{6,4},{7,5},{8,10},{9,11},{10,... | collective-permute-start | bytes 1179656 | tf_op jit(solution)/shard_map/ppermute | solution.py:47
  67.0 2.7 %collective-permute-start.18 = (bf16[272,256]{1,0:T(8,128)(2,1)S(1)}, bf16[272,256]{1,0:T(8,128)(2,1)S(1)}, u32[]{:S(2)}, u32[]{:S(2)}) collective-permute-start(bf16[272,256]{1,0:T(8,128)(2,1)S(1)} %chain_step.6.refs_0_), channel_id=1, source_target_pairs={{0,16},{4,20},{8,24},{12,28},{16,0},{20,4},{24,8},{28,12},{1,17},{... | collective-permute-start | bytes 417800 | tf_op jit(solution)/shard_map/ppermute | solution.py:47
  69.7 3.5 %project.4 = (f32[96,4096]{1,0:T(8,128)S(1)}, bf16[96,4096]{1,0:T(8,128)(2,1)S(1)}) custom-call(bf16[272,256]{1,0:T(8,128)(2,1)S(1)} %chain_step.6.refs_0_, bf16[2,96,1024]{2,1,0:T(8,128)(2,1)S(1)} %get-tuple-element.76.refs_0_.refs_1_, bf16[2,96,1024]{2,1,0:T(8,128)(2,1)S(1)} %collective-permute-done.15.refs_2_, bf16[1024,4096]{1,0:T(8,128)(2,1)S(1)} %bitcast.5, ...), custom_call_target="tpu_custom_call" | custom-call | flops 6000000000 | tf_op jit(solution)/shard_map/project/pallas_call | solution.py:434
  74.8 1.7 %collective-permute-done.18.refs_6_ = bf16[272,256]{1,0:T(8,128)(2,1)S(1)} collective-permute-done((bf16[272,256]{1,0:T(8,128)(2,1)S(1)}, bf16[272,256]{1,0:T(8,128)(2,1)S(1)}, u32[]{:S(2)}, u32[]{:S(2)}) %collective-permute-start.18) | collective-permute-done | bytes 139296 | tf_op jit(solution)/shard_map/ppermute | solution.py:47
  80.9 3.4 %attend_local.5 = (bf16[8,384,256]{2,1,0:T(8,128)(2,1)S(1)}, f32[8,384,256]{2,1,0:T(8,128)S(1)}) custom-call(bf16[272,256]{1,0:T(8,128)(2,1)S(1)} %get-tuple-element.83.refs_0_.refs_4_, s32[3]{0:T(128)S(1)} %copy-done, bf16[8,256,256]{2,1,0:T(8,128)(2,1)S(1)} %integer_maps.1.refs_1_.refs_2_, bf16[8,192,256]{2,1,0:T(8,128)(2,1)S(1)} %get-tuple-element.59.refs_0_.refs_3_, ...), custom_call_target="tpu_custom_call" | custom-call | flops 3000000000 | tf_op jit(solution)/shard_map/attend_local/pallas_call | solution.py:320
  85.0 1.9 %collective-permute-done.22.refs_7_ = bf16[272,256]{1,0:T(8,128)(2,1)S(1)} collective-permute-done((bf16[272,256]{1,0:T(8,128)(2,1)S(1)}, bf16[272,256]{1,0:T(8,128)(2,1)S(1)}, u32[]{:S(2)}, u32[]{:S(2)}) %collective-permute-start.22) | collective-permute-done | bytes 139296 | tf_op jit(solution)/shard_map/ppermute | solution.py:47
  91.5 1.6 %collective-permute-done.17.refs_1_ = bf16[96,4096]{1,0:T(8,128)(2,1)S(1)} collective-permute-done((bf16[96,4096]{1,0:T(8,128)(2,1)S(1)}, bf16[96,4096]{1,0:T(8,128)(2,1)S(1)}, u32[]{:S(2)}, u32[]{:S(2)}) %collective-permute-start.17) | collective-permute-done | bytes 786464 | tf_op jit(solution)/shard_map/ppermute | solution.py:47
  94.6 2.0 %collective-permute-start.25 = (bf16[96,1536]{1,0:T(8,128)(2,1)S(1)}, bf16[96,1536]{1,0:T(8,128)(2,1)S(1)}, u32[]{:S(2)}, u32[]{:S(2)}) collective-permute-start(bf16[96,1536]{1,0:T(8,128)(2,1)S(1)} %get-tuple-element.96), channel_id=1, source_target_pairs={{0,2},{1,3},{2,0},{3,1},{4,6},{5,7},{6,4},{7,5},{8,10},{9,11},{10,... | collective-permute-start | bytes 884744 | tf_op jit(solution)/shard_map/ppermute | solution.py:47
  97.3 5.7 %collective-permute-done.24.refs_3_ = bf16[96,2048]{1,0:T(8,128)(2,1)S(1)} collective-permute-done((bf16[96,2048]{1,0:T(8,128)(2,1)S(1)}, bf16[96,2048]{1,0:T(8,128)(2,1)S(1)}, u32[]{:S(2)}, u32[]{:S(2)}) %collective-permute-start.24) | collective-permute-done | bytes 393248 | tf_op jit(solution)/shard_map/ppermute | solution.py:47
  103.0 6.3 %collective-permute-done.25.refs_5_ = bf16[96,1536]{1,0:T(8,128)(2,1)S(1)} collective-permute-done((bf16[96,1536]{1,0:T(8,128)(2,1)S(1)}, bf16[96,1536]{1,0:T(8,128)(2,1)S(1)}, u32[]{:S(2)}, u32[]{:S(2)}) %collective-permute-start.25) | collective-permute-done | bytes 294944 | tf_op jit(solution)/shard_map/ppermute | solution.py:47
  (78 shorter events, 36.7 us)
Async XLA Ops:
  4.7 12.5 %collective-permute-start = (bf16[1,10,96,1024]{3,2,1,0:T(8,128)(2,1)}, bf16[1,10,96,1024]{3,2,1,0:T(8,128)(2,1)S(1)}, u32[]{:S(2)}, u32[]{:S(2)}) collective-permute-start(bf16[1,10,96,1024]{3,2,1,0:T(8,128)(2,1)} %get-tuple-element.52), channel_id=1, source_target_pairs={{0,1},{1,0},{2,3},{3,2},{4,5},{5,4},{6,7},{7,6},{8,9},{9,8},{10,11... | collective-permute-start | bytes 5898248 | tf_op jit(solution)/shard_map/ppermute | solution.py:47
  5.2 15.2 %collective-permute-start.1 = (bf16[1,2,96,1024]{3,2,1,0:T(8,128)(2,1)}, bf16[1,2,96,1024]{3,2,1,0:T(8,128)(2,1)}, u32[]{:S(2)}, u32[]{:S(2)}) collective-permute-start(bf16[1,2,96,1024]{3,2,1,0:T(8,128)(2,1)} %get-tuple-element.55), channel_id=1, source_target_pairs={{0,2},{1,3},{2,0},{3,1},{4,6},{5,7},{6,4},{7,5},{8,10},{9,11},{10,... | collective-permute-start | bytes 1179656 | tf_op jit(solution)/shard_map/ppermute | solution.py:47
  7.8 18.2 %collective-permute-start.2 = (bf16[1,2,96,1024]{3,2,1,0:T(8,128)(2,1)}, bf16[1,2,96,1024]{3,2,1,0:T(8,128)(2,1)}, u32[]{:S(2)}, u32[]{:S(2)}) collective-permute-start(bf16[1,2,96,1024]{3,2,1,0:T(8,128)(2,1)} %get-tuple-element.56), channel_id=1, source_target_pairs={{0,3},{1,2},{2,1},{3,0},{4,7},{5,6},{6,5},{7,4},{8,11},{9,10},{10,... | collective-permute-start | bytes 1179656 | tf_op jit(solution)/shard_map/ppermute | solution.py:47
  28.4 41.3 %collective-permute-start.16 = (bf16[1024,4096]{1,0:T(8,128)(2,1)S(1)}, bf16[1024,4096]{1,0:T(8,128)(2,1)S(1)}, u32[]{:S(2)}, u32[]{:S(2)}) collective-permute-start(bf16[1024,4096]{1,0:T(8,128)(2,1)S(1)} %later_than.1), channel_id=1, source_target_pairs={{0,1},{1,0},{2,3},{3,2},{4,5},{5,4},{6,7},{7,6},{8,9},{9,8},{10,11... | collective-permute-start | bytes 25165832 | tf_op jit(solution)/shard_map/ppermute | solution.py:47
  28.6 24.2 %collective-permute-start.7 = (bf16[2,2,96,1024]{3,2,1,0:T(8,128)(2,1)S(1)}, bf16[2,2,96,1024]{3,2,1,0:T(8,128)(2,1)S(1)}, u32[]{:S(2)}, u32[]{:S(2)}) collective-permute-start(bf16[2,2,96,1024]{3,2,1,0:T(8,128)(2,1)S(1)} %get-tuple-element.66), channel_id=1, source_target_pairs={{0,2},{1,3},{2,0},{3,1},{4,6},{5,7},{6,4},{7,5},{8,10},{9,11},{10,... | collective-permute-start | bytes 2359304 | tf_op jit(solution)/shard_map/ppermute | solution.py:47
  31.8 6.6 %collective-permute-start.4 = (bf16[272,256]{1,0:T(8,128)(2,1)S(1)}, bf16[272,256]{1,0:T(8,128)(2,1)S(1)}, u32[]{:S(2)}, u32[]{:S(2)}) collective-permute-start(bf16[272,256]{1,0:T(8,128)(2,1)S(1)} %get-tuple-element.61), channel_id=1, source_target_pairs={{0,8},{4,12},{8,0},{12,4},{16,24},{20,28},{24,16},{28,20},{1,9},{5... | collective-permute-start | bytes 417800 | tf_op jit(solution)/shard_map/ppermute | solution.py:47
  33.4 6.6 %collective-permute-start.5 = (bf16[272,256]{1,0:T(8,128)(2,1)S(1)}, bf16[272,256]{1,0:T(8,128)(2,1)S(1)}, u32[]{:S(2)}, u32[]{:S(2)}) collective-permute-start(bf16[272,256]{1,0:T(8,128)(2,1)S(1)} %get-tuple-element.62), channel_id=1, source_target_pairs={{0,12},{4,8},{8,4},{12,0},{16,28},{20,24},{24,20},{28,16},{1,13},{... | collective-permute-start | bytes 417800 | tf_op jit(solution)/shard_map/ppermute | solution.py:47
  35.8 21.0 %collective-permute-start.8 = (bf16[2,1,96,1024]{3,2,1,0:T(8,128)(2,1)S(1)}, bf16[2,1,96,1024]{3,2,1,0:T(8,128)(2,1)S(1)}, u32[]{:S(2)}, u32[]{:S(2)}) collective-permute-start(bf16[2,1,96,1024]{3,2,1,0:T(8,128)(2,1)S(1)} %get-tuple-element.69), channel_id=1, source_target_pairs={{0,2},{1,3},{2,0},{3,1},{4,6},{5,7},{6,4},{7,5},{8,10},{9,11},{10,... | collective-permute-start | bytes 1179656 | tf_op jit(solution)/shard_map/ppermute | solution.py:47
  40.6 8.8 %collective-permute-start.6 = (bf16[272,256]{1,0:T(8,128)(2,1)S(1)}, bf16[272,256]{1,0:T(8,128)(2,1)S(1)}, u32[]{:S(2)}, u32[]{:S(2)}) collective-permute-start(bf16[272,256]{1,0:T(8,128)(2,1)S(1)} %chain_step.4.refs_0_), channel_id=1, source_target_pairs={{0,16},{4,20},{8,24},{12,28},{16,0},{20,4},{24,8},{28,12},{1,17},{... | collective-permute-start | bytes 417800 | tf_op jit(solution)/shard_map/ppermute | solution.py:47
  50.2 8.2 %collective-permute-start.10 = (bf16[272,256]{1,0:T(8,128)(2,1)S(1)}, bf16[272,256]{1,0:T(8,128)(2,1)S(1)}, u32[]{:S(2)}, u32[]{:S(2)}) collective-permute-start(bf16[272,256]{1,0:T(8,128)(2,1)S(1)} %get-tuple-element.74), channel_id=1, source_target_pairs={{0,8},{4,12},{8,0},{12,4},{16,24},{20,28},{24,16},{28,20},{1,9},{5... | collective-permute-start | bytes 417800 | tf_op jit(solution)/shard_map/ppermute | solution.py:47
  50.6 9.3 %collective-permute-start.11 = (bf16[272,256]{1,0:T(8,128)(2,1)S(1)}, bf16[272,256]{1,0:T(8,128)(2,1)S(1)}, u32[]{:S(2)}, u32[]{:S(2)}) collective-permute-start(bf16[272,256]{1,0:T(8,128)(2,1)S(1)} %get-tuple-element.75), channel_id=1, source_target_pairs={{0,12},{4,8},{8,4},{12,0},{16,28},{20,24},{24,20},{28,16},{1,13},{... | collective-permute-start | bytes 417800 | tf_op jit(solution)/shard_map/ppermute | solution.py:47
  52.8 10.2 %collective-permute-start.9 = (bf16[272,256]{1,0:T(8,128)(2,1)S(1)}, bf16[272,256]{1,0:T(8,128)(2,1)S(1)}, u32[]{:S(2)}, u32[]{:S(2)}) collective-permute-start(bf16[272,256]{1,0:T(8,128)(2,1)S(1)} %get-tuple-element.73), channel_id=1, source_target_pairs={{0,4},{4,0},{8,12},{12,8},{16,20},{20,16},{24,28},{28,24},{1,5},{5... | collective-permute-start | bytes 417800 | tf_op jit(solution)/shard_map/ppermute | solution.py:47
  56.8 7.7 %collective-permute-start.12 = (bf16[272,256]{1,0:T(8,128)(2,1)S(1)}, bf16[272,256]{1,0:T(8,128)(2,1)S(1)}, u32[]{:S(2)}, u32[]{:S(2)}) collective-permute-start(bf16[272,256]{1,0:T(8,128)(2,1)S(1)} %get-tuple-element.77), channel_id=1, source_target_pairs={{0,4},{4,0},{8,12},{12,8},{16,20},{20,16},{24,28},{28,24},{1,5},{5... | collective-permute-start | bytes 417800 | tf_op jit(solution)/shard_map/ppermute | solution.py:47
  58.4 7.8 %collective-permute-start.13 = (bf16[272,256]{1,0:T(8,128)(2,1)S(1)}, bf16[272,256]{1,0:T(8,128)(2,1)S(1)}, u32[]{:S(2)}, u32[]{:S(2)}) collective-permute-start(bf16[272,256]{1,0:T(8,128)(2,1)S(1)} %get-tuple-element.78), channel_id=1, source_target_pairs={{0,8},{4,12},{8,0},{12,4},{16,24},{20,28},{24,16},{28,20},{1,9},{5... | collective-permute-start | bytes 417800 | tf_op jit(solution)/shard_map/ppermute | solution.py:47
  60.0 6.4 %collective-permute-start.14 = (bf16[272,256]{1,0:T(8,128)(2,1)S(1)}, bf16[272,256]{1,0:T(8,128)(2,1)S(1)}, u32[]{:S(2)}, u32[]{:S(2)}) collective-permute-start(bf16[272,256]{1,0:T(8,128)(2,1)S(1)} %get-tuple-element.79), channel_id=1, source_target_pairs={{0,12},{4,8},{8,4},{12,0},{16,28},{20,24},{24,20},{28,16},{1,13},{... | collective-permute-start | bytes 417800 | tf_op jit(solution)/shard_map/ppermute | solution.py:47
  64.6 16.4 %collective-permute-start.19 = (bf16[2,1,96,1024]{3,2,1,0:T(8,128)(2,1)}, bf16[2,1,96,1024]{3,2,1,0:T(8,128)(2,1)S(1)}, u32[]{:S(2)}, u32[]{:S(2)}) collective-permute-start(bf16[2,1,96,1024]{3,2,1,0:T(8,128)(2,1)} %get-tuple-element.85), channel_id=1, source_target_pairs={{0,2},{1,3},{2,0},{3,1},{4,6},{5,7},{6,4},{7,5},{8,10},{9,11},{10,... | collective-permute-start | bytes 1179656 | tf_op jit(solution)/shard_map/ppermute | solution.py:47
  67.0 9.5 %collective-permute-start.18 = (bf16[272,256]{1,0:T(8,128)(2,1)S(1)}, bf16[272,256]{1,0:T(8,128)(2,1)S(1)}, u32[]{:S(2)}, u32[]{:S(2)}) collective-permute-start(bf16[272,256]{1,0:T(8,128)(2,1)S(1)} %chain_step.6.refs_0_), channel_id=1, source_target_pairs={{0,16},{4,20},{8,24},{12,28},{16,0},{20,4},{24,8},{28,12},{1,17},{... | collective-permute-start | bytes 417800 | tf_op jit(solution)/shard_map/ppermute | solution.py:47
  73.2 20.0 %collective-permute-start.17 = (bf16[96,4096]{1,0:T(8,128)(2,1)S(1)}, bf16[96,4096]{1,0:T(8,128)(2,1)S(1)}, u32[]{:S(2)}, u32[]{:S(2)}) collective-permute-start(bf16[96,4096]{1,0:T(8,128)(2,1)S(1)} %get-tuple-element.82), channel_id=1, source_target_pairs={{0,2},{1,3},{2,0},{3,1},{4,6},{5,7},{6,4},{7,5},{8,10},{9,11},{10,... | collective-permute-start | bytes 2359304 | tf_op jit(solution)/shard_map/ppermute | solution.py:47
  77.4 7.0 %collective-permute-start.20 = (bf16[272,256]{1,0:T(8,128)(2,1)S(1)}, bf16[272,256]{1,0:T(8,128)(2,1)S(1)}, u32[]{:S(2)}, u32[]{:S(2)}) collective-permute-start(bf16[272,256]{1,0:T(8,128)(2,1)S(1)} %get-tuple-element.88), channel_id=1, source_target_pairs={{0,4},{4,0},{8,12},{12,8},{16,20},{20,16},{24,28},{28,24},{1,5},{5... | collective-permute-start | bytes 417800 | tf_op jit(solution)/shard_map/ppermute | solution.py:47
  78.9 6.1 %collective-permute-start.21 = (bf16[272,256]{1,0:T(8,128)(2,1)S(1)}, bf16[272,256]{1,0:T(8,128)(2,1)S(1)}, u32[]{:S(2)}, u32[]{:S(2)}) collective-permute-start(bf16[272,256]{1,0:T(8,128)(2,1)S(1)} %get-tuple-element.89), channel_id=1, source_target_pairs={{0,8},{4,12},{8,0},{12,4},{16,24},{20,28},{24,16},{28,20},{1,9},{5... | collective-permute-start | bytes 417800 | tf_op jit(solution)/shard_map/ppermute | solution.py:47
  79.6 7.3 %collective-permute-start.22 = (bf16[272,256]{1,0:T(8,128)(2,1)S(1)}, bf16[272,256]{1,0:T(8,128)(2,1)S(1)}, u32[]{:S(2)}, u32[]{:S(2)}) collective-permute-start(bf16[272,256]{1,0:T(8,128)(2,1)S(1)} %get-tuple-element.90), channel_id=1, source_target_pairs={{0,12},{4,8},{8,4},{12,0},{16,28},{20,24},{24,20},{28,16},{1,13},{... | collective-permute-start | bytes 417800 | tf_op jit(solution)/shard_map/ppermute | solution.py:47
  91.0 12.0 %collective-permute-start.24 = (bf16[96,2048]{1,0:T(8,128)(2,1)S(1)}, bf16[96,2048]{1,0:T(8,128)(2,1)S(1)}, u32[]{:S(2)}, u32[]{:S(2)}) collective-permute-start(bf16[96,2048]{1,0:T(8,128)(2,1)S(1)} %get-tuple-element.94), channel_id=1, source_target_pairs={{0,2},{1,3},{2,0},{3,1},{4,6},{5,7},{6,4},{7,5},{8,10},{9,11},{10,... | collective-permute-start | bytes 1179656 | tf_op jit(solution)/shard_map/ppermute | solution.py:47
  94.6 14.8 %collective-permute-start.25 = (bf16[96,1536]{1,0:T(8,128)(2,1)S(1)}, bf16[96,1536]{1,0:T(8,128)(2,1)S(1)}, u32[]{:S(2)}, u32[]{:S(2)}) collective-permute-start(bf16[96,1536]{1,0:T(8,128)(2,1)S(1)} %get-tuple-element.96), channel_id=1, source_target_pairs={{0,2},{1,3},{2,0},{3,1},{4,6},{5,7},{6,4},{7,5},{8,10},{9,11},{10,... | collective-permute-start | bytes 884744 | tf_op jit(solution)/shard_map/ppermute | solution.py:47
  97.2 13.5 %collective-permute-start.26 = (bf16[96,512]{1,0:T(8,128)(2,1)S(1)}, bf16[96,512]{1,0:T(8,128)(2,1)S(1)}, u32[]{:S(2)}, u32[]{:S(2)}) collective-permute-start(bf16[96,512]{1,0:T(8,128)(2,1)S(1)} %get-tuple-element.98), channel_id=1, source_target_pairs={{0,2},{1,3},{2,0},{3,1},{4,6},{5,7},{6,4},{7,5},{8,10},{9,11},{10,... | collective-permute-start | bytes 294920 | tf_op jit(solution)/shard_map/ppermute | solution.py:47
  (12 other events, 78.5 us)

commit v3 on v2

--- a/solution.py
+++ b/solution.py
@@ -104,12 +104,13 @@
         out_ref[i] = jnp.exp(product * scales[i]).astype(bf16)
 
 
-def pack_kernel(places, arrays, where_ref, *refs):
+def pack_kernel(places, arrays, *refs):
+    me = lax.axis_index("head")
     ins, outs, sems = refs[:arrays], refs[arrays:-1], refs[-1]
     copies = []
     for n, (which, first, second, k, out, i, j, count) in enumerate(places):
         width = outs[out].shape[-1]
-        start = 0 if k is None else pl.multiple_of((where_ref[0] ^ k) * width, width)
+        start = 0 if k is None else pl.multiple_of((me ^ k) * width, width)
         source = ins[which].at[first, pl.ds(second, count), :, pl.ds(start, width)]
         copies.append(pltpu.make_async_copy(source, outs[out].at[i, pl.ds(j, count)], sems.at[n]))
     for copy in copies:
@@ -118,7 +119,7 @@
         copy.wait()
 
 
-def pack(where, wanted, shape, mebibytes):
+def pack(wanted, shape, mebibytes):
     arrays, places, shapes = [], [], []
     for out, table in enumerate(wanted):
         shapes.append((len(table), len(table[0]), *shape))
@@ -135,14 +136,13 @@
     return pl.pallas_call(
         functools.partial(pack_kernel, places, len(arrays)),
         out_shape=[jax.ShapeDtypeStruct(shape, bf16) for shape in shapes],
-        in_specs=[pl.BlockSpec(memory_space=pltpu.SMEM)]
-        + [pl.BlockSpec(memory_space=pl.ANY)] * len(arrays),
+        in_specs=waits(arrays),
         out_specs=[pl.BlockSpec(memory_space=pltpu.VMEM)] * len(shapes),
         scratch_shapes=[pltpu.SemaphoreType.DMA((len(places),))],
         compiler_params=params(mebibytes),
         cost_estimate=busy(0),
         name="pack",
-    )(where, *arrays)
+    )(*arrays)
 
 
 def joined(refs, places, cut):
@@ -531,7 +531,7 @@
         if s > 0 or kind == 0
     ]
     straight = [[[(x, 0, kind, k) for kind in (1, 2)]] for k in range(2, partners)]
-    *first, near = pack(where, [*straight, [[(x, *entry) for entry in beside]]], shape, 60)
+    *first, near = pack([*straight, [[(x, *entry) for entry in beside]]], shape, 60)
     first = [swap(value, "head", k + 2) for k, value in enumerate(first)]
     near = swap(near, "head", 1)
     messages = [(s, (1, 2)) for s in range(1, seqs)] + [(s, (0,)) for s in range(seqs)]
@@ -544,7 +544,7 @@
         for k in outer
     ]
     wanted.append([[(x, s, kind, 0) for kind in (0, 1, 2)] for s in range(seqs)])
-    *packed, own_rows = pack(where, wanted, shape, 20)
+    *packed, own_rows = pack(wanted, shape, 20)
     packed = [swap(value, "head", k) for value, k in zip(packed, list(outer) * len(messages))]
     packed = [packed[n * len(outer) : (n + 1) * len(outer)] for n in range(len(messages))]
     asked = packed[seqs - 1 :]

time: 112 us -> 109 us (0.973)
  Pallas kernels: 36.5 us -> 32.4 us
  local copies, waits for them, and re-layouts: 8.75 us -> 10.2 us
    pallas_call x2, Pallas kernels: 6.39 us -> 4.27 us  [pack(): pl.pallas_call(functools.partial(pack_kernel, places, len(arrays)), out_s...]
    unnamed x20 -> x16, local copies, waits for them, and re-layouts: 8.75 us -> 10.2 us
    pallas_call x3, Pallas kernels: 8.7 us -> 7.54 us  [attend_local(): pl.pallas_call(ordered(functools.partial(local_kernel, first, q_at, v_at,...]
  transfers between devices with their start and end apart: 27 -> 27, of which waited for: 14 -> 14; matrix products, arithmetic and copies ran while one was open for 7% -> 7% of each run, Pallas kernels for 26% -> 25%
where the time goes in v3:
time: 109 us
  waiting for transfers between devices  34.2 us (31%)
  Pallas kernels  32.4 us (30%)
  starting transfers between devices  31.3 us (29%)
  local copies, waits for them, and re-layouts  10.2 us (9%)
    ppermute x27, waiting for transfers between devices, swap(): lax.ppermute(value, axis, [(j, j ^ bit) for j in range(lax.axis_size(axis...  34.2 us
    ppermute x27, starting transfers between devices, swap(): lax.ppermute(value, axis, [(j, j ^ bit) for j in range(lax.axis_size(axis...  31.3 us
    unnamed x16, local copies, waits for them, and re-layouts  10.2 us
    pallas_call x3, Pallas kernels, attend_local(): pl.pallas_call(ordered(functools.partial(local_kernel, first, q_at, v_at,...  7.54 us
    pallas_call x4, Pallas kernels, project(): pl.pallas_call(ordered(functools.partial(kernel, first, math.gcd(unit, 51...  6.53 us
    pallas_call x2, Pallas kernels, pack(): pl.pallas_call(functools.partial(pack_kernel, places, len(arrays)), out_s...  4.27 us
    pallas_call x2, Pallas kernels, block_state(): pl.pallas_call(ordered(functools.partial(state_kernel, k_at, v_at, heads,...  3.09 us
    pallas_call x4, Pallas kernels, chain_step(): pl.pallas_call(ordered(functools.partial(step_kernel, levels), len(after)...  2.91 us
  transfers between devices with their start and end apart: 27, of which 14 were waited for; matrix products, arithmetic and copies ran while one was open for 7% of the time, Pallas kernels for 25%

profile of v3, /device:TPU:0, one launch (start us, length us, event | category | flops | bytes accessed | tf_op | source)
XLA Modules:
  0.0 108.5 jit_solution(12487410229156460013)
XLA Ops:
  0.0 3.3 %pack.2 = (bf16[1,2,96,1024]{3,2,1,0:T(8,128)(2,1)}, bf16[1,2,96,1024]{3,2,1,0:T(8,128)(2,1)}, bf16[1,10,96,1024]{3,2,1,0:T(8,128)(2,1)}) custom-call(bf16[2,3,96,4096]{3,2,1,0:T(8,128)(2,1)} %bitcast.8), custom_call_target="tpu_custom_call" | custom-call | tf_op jit(solution)/shard_map/pack/pallas_call | solution.py:136
  3.8 2.6 %collective-permute-start.1 = (bf16[1,2,96,1024]{3,2,1,0:T(8,128)(2,1)}, bf16[1,2,96,1024]{3,2,1,0:T(8,128)(2,1)S(1)}, u32[]{:S(2)}, u32[]{:S(2)}) collective-permute-start(bf16[1,2,96,1024]{3,2,1,0:T(8,128)(2,1)} %get-tuple-element.55), channel_id=1, source_target_pairs={{0,2},{1,3},{2,0},{3,1},{4,6},{5,7},{6,4},{7,5},{8,10},{9,11},{10,... | collective-permute-start | bytes 1179656 | tf_op jit(solution)/shard_map/ppermute | solution.py:47
  6.5 7.8 %copy.8.refs_0_ = bf16[1024,4096]{1,0:T(8,128)(2,1)} copy(bf16[1024,4096]{1,0:T(8,128)(2,1)} %refs_3_.3) | data formatting | bytes 16777216
  15.0 2.3 %copy-done = bf16[2,96,3,4096]{3,1,2,0:T(8,128)(2,1)S(1)} copy-done((bf16[2,96,3,4096]{3,1,2,0:T(8,128)(2,1)S(1)}, bf16[2,96,3,4096]{3,1,2,0:T(8,128)(2,1)}, u32[]{:S(2)}) %copy-start) | copy-done | bytes 4718616
  19.2 5.3 %collective-permute-done.2.refs_4_.refs_6_.refs_10_ = bf16[1,2,96,1024]{3,2,1,0:T(8,128)(2,1)S(1)} collective-permute-done((bf16[1,2,96,1024]{3,2,1,0:T(8,128)(2,1)}, bf16[1,2,96,1024]{3,2,1,0:T(8,128)(2,1)S(1)}, u32[]{:S(2)}, u32[]{:S(2)}) %collective-permute-start.2) | collective-permute-done | bytes 393248 | tf_op jit(solution)/shard_map/ppermute | solution.py:47
  26.3 1.7 %collective-permute-start.7 = (bf16[2,2,96,1024]{3,2,1,0:T(8,128)(2,1)S(1)}, bf16[2,2,96,1024]{3,2,1,0:T(8,128)(2,1)S(1)}, u32[]{:S(2)}, u32[]{:S(2)}) collective-permute-start(bf16[2,2,96,1024]{3,2,1,0:T(8,128)(2,1)S(1)} %get-tuple-element.66), channel_id=1, source_target_pairs={{0,2},{1,3},{2,0},{3,1},{4,6},{5,7},{6,4},{7,5},{8,10},{9,11},{10,... | collective-permute-start | bytes 2359304 | tf_op jit(solution)/shard_map/ppermute | solution.py:47
  29.5 1.6 %collective-permute-start.4 = (bf16[272,256]{1,0:T(8,128)(2,1)S(1)}, bf16[272,256]{1,0:T(8,128)(2,1)S(1)}, u32[]{:S(2)}, u32[]{:S(2)}) collective-permute-start(bf16[272,256]{1,0:T(8,128)(2,1)S(1)} %get-tuple-element.61), channel_id=1, source_target_pairs={{0,8},{4,12},{8,0},{12,4},{16,24},{20,28},{24,16},{28,20},{1,9},{5... | collective-permute-start | bytes 417800 | tf_op jit(solution)/shard_map/ppermute | solution.py:47
  34.1 2.1 %collective-permute-done.4.refs_4_ = bf16[272,256]{1,0:T(8,128)(2,1)S(1)} collective-permute-done((bf16[272,256]{1,0:T(8,128)(2,1)S(1)}, bf16[272,256]{1,0:T(8,128)(2,1)S(1)}, u32[]{:S(2)}, u32[]{:S(2)}) %collective-permute-start.4) | collective-permute-done | bytes 139296 | tf_op jit(solution)/shard_map/ppermute | solution.py:47
  36.1 1.6 %collective-permute-done.5.refs_5_ = bf16[272,256]{1,0:T(8,128)(2,1)S(1)} collective-permute-done((bf16[272,256]{1,0:T(8,128)(2,1)S(1)}, bf16[272,256]{1,0:T(8,128)(2,1)S(1)}, u32[]{:S(2)}, u32[]{:S(2)}) %collective-permute-start.5) | collective-permute-done | bytes 139296 | tf_op jit(solution)/shard_map/ppermute | solution.py:47
  38.3 2.7 %collective-permute-start.6 = (bf16[272,256]{1,0:T(8,128)(2,1)S(1)}, bf16[272,256]{1,0:T(8,128)(2,1)S(1)}, u32[]{:S(2)}, u32[]{:S(2)}) collective-permute-start(bf16[272,256]{1,0:T(8,128)(2,1)S(1)} %chain_step.4.refs_0_), channel_id=1, source_target_pairs={{0,16},{4,20},{8,24},{12,28},{16,0},{20,4},{24,8},{28,12},{1,17},{... | collective-permute-start | bytes 417800 | tf_op jit(solution)/shard_map/ppermute | solution.py:47
  41.0 2.1 %attend_local.3 = (bf16[8,192,256]{2,1,0:T(8,128)(2,1)S(1)}, f32[8,192,256]{2,1,0:T(8,128)S(1)}) custom-call(bf16[272,256]{1,0:T(8,128)(2,1)S(1)} %chain_step.4.refs_0_, s32[3]{0:T(128)S(1)} %pad_add_fusion.refs_1_, bf16[8,256,256]{2,1,0:T(8,128)(2,1)S(1)} %integer_maps.1.refs_1_.refs_2_, bf16[8,192,256]{2,1,0:T(8,128)(2,1)S(1)} %get-tuple-element.54.refs_0_.refs_3_, ...), custom_call_target="tpu_custom_call" | custom-call | flops 3000000000 | tf_op jit(solution)/shard_map/attend_local/pallas_call | solution.py:320
  43.1 4.0 %collective-permute-done.6.refs_6_ = bf16[272,256]{1,0:T(8,128)(2,1)S(1)} collective-permute-done((bf16[272,256]{1,0:T(8,128)(2,1)S(1)}, bf16[272,256]{1,0:T(8,128)(2,1)S(1)}, u32[]{:S(2)}, u32[]{:S(2)}) %collective-permute-start.6) | collective-permute-done | bytes 139296 | tf_op jit(solution)/shard_map/ppermute | solution.py:47
  48.3 2.2 %collective-permute-start.11 = (bf16[272,256]{1,0:T(8,128)(2,1)S(1)}, bf16[272,256]{1,0:T(8,128)(2,1)S(1)}, u32[]{:S(2)}, u32[]{:S(2)}) collective-permute-start(bf16[272,256]{1,0:T(8,128)(2,1)S(1)} %get-tuple-element.75), channel_id=1, source_target_pairs={{0,12},{4,8},{8,4},{12,0},{16,28},{20,24},{24,20},{28,16},{1,13},{... | collective-permute-start | bytes 417800 | tf_op jit(solution)/shard_map/ppermute | solution.py:47
  56.1 1.6 %collective-permute-start.13 = (bf16[272,256]{1,0:T(8,128)(2,1)S(1)}, bf16[272,256]{1,0:T(8,128)(2,1)S(1)}, u32[]{:S(2)}, u32[]{:S(2)}) collective-permute-start(bf16[272,256]{1,0:T(8,128)(2,1)S(1)} %get-tuple-element.78), channel_id=1, source_target_pairs={{0,8},{4,12},{8,0},{12,4},{16,24},{20,28},{24,16},{28,20},{1,9},{5... | collective-permute-start | bytes 417800 | tf_op jit(solution)/shard_map/ppermute | solution.py:47
  58.1 2.1 %attend_local.4 = (bf16[8,192,256]{2,1,0:T(8,128)(2,1)S(1)}, f32[8,192,256]{2,1,0:T(8,128)S(1)}) custom-call(f32[272,256]{1,0:T(8,128)S(1)} %get-tuple-element.68.refs_0_.refs_2_, s32[3]{0:T(128)S(1)} %pad_add_fusion.refs_1_, bf16[8,256,256]{2,1,0:T(8,128)(2,1)S(1)} %integer_maps.1.refs_1_.refs_2_, ...), custom_call_target="tpu_custom_call" | custom-call | flops 3000000000 | tf_op jit(solution)/shard_map/attend_local/pallas_call | solution.py:320
  61.7 1.6 %collective-permute-start.19 = (bf16[2,1,96,1024]{3,2,1,0:T(8,128)(2,1)S(1)}, bf16[2,1,96,1024]{3,2,1,0:T(8,128)(2,1)S(1)}, u32[]{:S(2)}, u32[]{:S(2)}) collective-permute-start(bf16[2,1,96,1024]{3,2,1,0:T(8,128)(2,1)S(1)} %get-tuple-element.85), channel_id=1, source_target_pairs={{0,2},{1,3},{2,0},{3,1},{4,6},{5,7},{6,4},{7,5},{8,10},{9,11},{10,... | collective-permute-start | bytes 1179656 | tf_op jit(solution)/shard_map/ppermute | solution.py:47
  64.7 2.7 %collective-permute-start.18 = (bf16[272,256]{1,0:T(8,128)(2,1)S(1)}, bf16[272,256]{1,0:T(8,128)(2,1)S(1)}, u32[]{:S(2)}, u32[]{:S(2)}) collective-permute-start(bf16[272,256]{1,0:T(8,128)(2,1)S(1)} %chain_step.6.refs_0_), channel_id=1, source_target_pairs={{0,16},{4,20},{8,24},{12,28},{16,0},{20,4},{24,8},{28,12},{1,17},{... | collective-permute-start | bytes 417800 | tf_op jit(solution)/shard_map/ppermute | solution.py:47
  67.4 3.5 %project.4 = (f32[96,4096]{1,0:T(8,128)S(1)}, bf16[96,4096]{1,0:T(8,128)(2,1)S(1)}) custom-call(bf16[272,256]{1,0:T(8,128)(2,1)S(1)} %chain_step.6.refs_0_, bf16[2,96,1024]{2,1,0:T(8,128)(2,1)S(1)} %get-tuple-element.76.refs_0_.refs_1_, bf16[2,96,1024]{2,1,0:T(8,128)(2,1)S(1)} %collective-permute-done.15.refs_2_, bf16[1024,4096]{1,0:T(8,128)(2,1)S(1)} %bitcast.5, ...), custom_call_target="tpu_custom_call" | custom-call | flops 6000000000 | tf_op jit(solution)/shard_map/project/pallas_call | solution.py:434
  70.9 1.6 %collective-permute-start.17 = (bf16[96,4096]{1,0:T(8,128)(2,1)S(1)}, bf16[96,4096]{1,0:T(8,128)(2,1)S(1)}, u32[]{:S(2)}, u32[]{:S(2)}) collective-permute-start(bf16[96,4096]{1,0:T(8,128)(2,1)S(1)} %get-tuple-element.82), channel_id=1, source_target_pairs={{0,2},{1,3},{2,0},{3,1},{4,6},{5,7},{6,4},{7,5},{8,10},{9,11},{10,... | collective-permute-start | bytes 2359304 | tf_op jit(solution)/shard_map/ppermute | solution.py:47
  78.0 3.4 %attend_local.5 = (bf16[8,384,256]{2,1,0:T(8,128)(2,1)S(1)}, f32[8,384,256]{2,1,0:T(8,128)S(1)}) custom-call(bf16[272,256]{1,0:T(8,128)(2,1)S(1)} %get-tuple-element.83.refs_0_.refs_4_, s32[3]{0:T(128)S(1)} %pad_add_fusion.refs_1_, bf16[8,256,256]{2,1,0:T(8,128)(2,1)S(1)} %integer_maps.1.refs_1_.refs_2_, ...), custom_call_target="tpu_custom_call" | custom-call | flops 3000000000 | tf_op jit(solution)/shard_map/attend_local/pallas_call | solution.py:320
  81.8 2.2 %collective-permute-done.22.refs_7_ = bf16[272,256]{1,0:T(8,128)(2,1)S(1)} collective-permute-done((bf16[272,256]{1,0:T(8,128)(2,1)S(1)}, bf16[272,256]{1,0:T(8,128)(2,1)S(1)}, u32[]{:S(2)}, u32[]{:S(2)}) %collective-permute-start.22) | collective-permute-done | bytes 139296 | tf_op jit(solution)/shard_map/ppermute | solution.py:47
  91.5 1.6 %collective-permute-start.25 = (bf16[96,1536]{1,0:T(8,128)(2,1)S(1)}, bf16[96,1536]{1,0:T(8,128)(2,1)S(1)}, u32[]{:S(2)}, u32[]{:S(2)}) collective-permute-start(bf16[96,1536]{1,0:T(8,128)(2,1)S(1)} %get-tuple-element.96), channel_id=1, source_target_pairs={{0,2},{1,3},{2,0},{3,1},{4,6},{5,7},{6,4},{7,5},{8,10},{9,11},{10,... | collective-permute-start | bytes 884744 | tf_op jit(solution)/shard_map/ppermute | solution.py:47
  94.3 5.8 %collective-permute-done.24.refs_3_ = bf16[96,2048]{1,0:T(8,128)(2,1)S(1)} collective-permute-done((bf16[96,2048]{1,0:T(8,128)(2,1)S(1)}, bf16[96,2048]{1,0:T(8,128)(2,1)S(1)}, u32[]{:S(2)}, u32[]{:S(2)}) %collective-permute-start.24) | collective-permute-done | bytes 393248 | tf_op jit(solution)/shard_map/ppermute | solution.py:47
  100.1 6.3 %collective-permute-done.25.refs_5_ = bf16[96,1536]{1,0:T(8,128)(2,1)S(1)} collective-permute-done((bf16[96,1536]{1,0:T(8,128)(2,1)S(1)}, bf16[96,1536]{1,0:T(8,128)(2,1)S(1)}, u32[]{:S(2)}, u32[]{:S(2)}) %collective-permute-start.25) | collective-permute-done | bytes 294944 | tf_op jit(solution)/shard_map/ppermute | solution.py:47
  (73 shorter events, 36.6 us)
Async XLA Ops:
  3.3 11.6 %collective-permute-start = (bf16[1,10,96,1024]{3,2,1,0:T(8,128)(2,1)}, bf16[1,10,96,1024]{3,2,1,0:T(8,128)(2,1)S(1)}, u32[]{:S(2)}, u32[]{:S(2)}) collective-permute-start(bf16[1,10,96,1024]{3,2,1,0:T(8,128)(2,1)} %get-tuple-element.52), channel_id=1, source_target_pairs={{0,1},{1,0},{2,3},{3,2},{4,5},{5,4},{6,7},{7,6},{8,9},{9,8},{10,11... | collective-permute-start | bytes 5898248 | tf_op jit(solution)/shard_map/ppermute | solution.py:47
  3.8 15.4 %collective-permute-start.1 = (bf16[1,2,96,1024]{3,2,1,0:T(8,128)(2,1)}, bf16[1,2,96,1024]{3,2,1,0:T(8,128)(2,1)S(1)}, u32[]{:S(2)}, u32[]{:S(2)}) collective-permute-start(bf16[1,2,96,1024]{3,2,1,0:T(8,128)(2,1)} %get-tuple-element.55), channel_id=1, source_target_pairs={{0,2},{1,3},{2,0},{3,1},{4,6},{5,7},{6,4},{7,5},{8,10},{9,11},{10,... | collective-permute-start | bytes 1179656 | tf_op jit(solution)/shard_map/ppermute | solution.py:47
  6.4 18.1 %collective-permute-start.2 = (bf16[1,2,96,1024]{3,2,1,0:T(8,128)(2,1)}, bf16[1,2,96,1024]{3,2,1,0:T(8,128)(2,1)S(1)}, u32[]{:S(2)}, u32[]{:S(2)}) collective-permute-start(bf16[1,2,96,1024]{3,2,1,0:T(8,128)(2,1)} %get-tuple-element.56), channel_id=1, source_target_pairs={{0,3},{1,2},{2,1},{3,0},{4,7},{5,6},{6,5},{7,4},{8,11},{9,10},{10,... | collective-permute-start | bytes 1179656 | tf_op jit(solution)/shard_map/ppermute | solution.py:47
  26.1 41.3 %collective-permute-start.16 = (bf16[1024,4096]{1,0:T(8,128)(2,1)S(1)}, bf16[1024,4096]{1,0:T(8,128)(2,1)S(1)}, u32[]{:S(2)}, u32[]{:S(2)}) collective-permute-start(bf16[1024,4096]{1,0:T(8,128)(2,1)S(1)} %later_than.1), channel_id=1, source_target_pairs={{0,1},{1,0},{2,3},{3,2},{4,5},{5,4},{6,7},{7,6},{8,9},{9,8},{10,11... | collective-permute-start | bytes 25165832 | tf_op jit(solution)/shard_map/ppermute | solution.py:47
  26.3 24.2 %collective-permute-start.7 = (bf16[2,2,96,1024]{3,2,1,0:T(8,128)(2,1)S(1)}, bf16[2,2,96,1024]{3,2,1,0:T(8,128)(2,1)S(1)}, u32[]{:S(2)}, u32[]{:S(2)}) collective-permute-start(bf16[2,2,96,1024]{3,2,1,0:T(8,128)(2,1)S(1)} %get-tuple-element.66), channel_id=1, source_target_pairs={{0,2},{1,3},{2,0},{3,1},{4,6},{5,7},{6,4},{7,5},{8,10},{9,11},{10,... | collective-permute-start | bytes 2359304 | tf_op jit(solution)/shard_map/ppermute | solution.py:47
  29.5 6.6 %collective-permute-start.4 = (bf16[272,256]{1,0:T(8,128)(2,1)S(1)}, bf16[272,256]{1,0:T(8,128)(2,1)S(1)}, u32[]{:S(2)}, u32[]{:S(2)}) collective-permute-start(bf16[272,256]{1,0:T(8,128)(2,1)S(1)} %get-tuple-element.61), channel_id=1, source_target_pairs={{0,8},{4,12},{8,0},{12,4},{16,24},{20,28},{24,16},{28,20},{1,9},{5... | collective-permute-start | bytes 417800 | tf_op jit(solution)/shard_map/ppermute | solution.py:47
  31.1 6.6 %collective-permute-start.5 = (bf16[272,256]{1,0:T(8,128)(2,1)S(1)}, bf16[272,256]{1,0:T(8,128)(2,1)S(1)}, u32[]{:S(2)}, u32[]{:S(2)}) collective-permute-start(bf16[272,256]{1,0:T(8,128)(2,1)S(1)} %get-tuple-element.62), channel_id=1, source_target_pairs={{0,12},{4,8},{8,4},{12,0},{16,28},{20,24},{24,20},{28,16},{1,13},{... | collective-permute-start | bytes 417800 | tf_op jit(solution)/shard_map/ppermute | solution.py:47
  33.6 21.0 %collective-permute-start.8 = (bf16[2,1,96,1024]{3,2,1,0:T(8,128)(2,1)S(1)}, bf16[2,1,96,1024]{3,2,1,0:T(8,128)(2,1)S(1)}, u32[]{:S(2)}, u32[]{:S(2)}) collective-permute-start(bf16[2,1,96,1024]{3,2,1,0:T(8,128)(2,1)S(1)} %get-tuple-element.69), channel_id=1, source_target_pairs={{0,2},{1,3},{2,0},{3,1},{4,6},{5,7},{6,4},{7,5},{8,10},{9,11},{10,... | collective-permute-start | bytes 1179656 | tf_op jit(solution)/shard_map/ppermute | solution.py:47
  38.3 8.8 %collective-permute-start.6 = (bf16[272,256]{1,0:T(8,128)(2,1)S(1)}, bf16[272,256]{1,0:T(8,128)(2,1)S(1)}, u32[]{:S(2)}, u32[]{:S(2)}) collective-permute-start(bf16[272,256]{1,0:T(8,128)(2,1)S(1)} %chain_step.4.refs_0_), channel_id=1, source_target_pairs={{0,16},{4,20},{8,24},{12,28},{16,0},{20,4},{24,8},{28,12},{1,17},{... | collective-permute-start | bytes 417800 | tf_op jit(solution)/shard_map/ppermute | solution.py:47
  48.0 8.2 %collective-permute-start.10 = (bf16[272,256]{1,0:T(8,128)(2,1)S(1)}, bf16[272,256]{1,0:T(8,128)(2,1)S(1)}, u32[]{:S(2)}, u32[]{:S(2)}) collective-permute-start(bf16[272,256]{1,0:T(8,128)(2,1)S(1)} %get-tuple-element.74), channel_id=1, source_target_pairs={{0,8},{4,12},{8,0},{12,4},{16,24},{20,28},{24,16},{28,20},{1,9},{5... | collective-permute-start | bytes 417800 | tf_op jit(solution)/shard_map/ppermute | solution.py:47
  48.3 9.3 %collective-permute-start.11 = (bf16[272,256]{1,0:T(8,128)(2,1)S(1)}, bf16[272,256]{1,0:T(8,128)(2,1)S(1)}, u32[]{:S(2)}, u32[]{:S(2)}) collective-permute-start(bf16[272,256]{1,0:T(8,128)(2,1)S(1)} %get-tuple-element.75), channel_id=1, source_target_pairs={{0,12},{4,8},{8,4},{12,0},{16,28},{20,24},{24,20},{28,16},{1,13},{... | collective-permute-start | bytes 417800 | tf_op jit(solution)/shard_map/ppermute | solution.py:47
  50.5 9.6 %collective-permute-start.9 = (bf16[272,256]{1,0:T(8,128)(2,1)S(1)}, bf16[272,256]{1,0:T(8,128)(2,1)S(1)}, u32[]{:S(2)}, u32[]{:S(2)}) collective-permute-start(bf16[272,256]{1,0:T(8,128)(2,1)S(1)} %get-tuple-element.73), channel_id=1, source_target_pairs={{0,4},{4,0},{8,12},{12,8},{16,20},{20,16},{24,28},{28,24},{1,5},{5... | collective-permute-start | bytes 417800 | tf_op jit(solution)/shard_map/ppermute | solution.py:47
  54.6 7.1 %collective-permute-start.12 = (bf16[272,256]{1,0:T(8,128)(2,1)S(1)}, bf16[272,256]{1,0:T(8,128)(2,1)S(1)}, u32[]{:S(2)}, u32[]{:S(2)}) collective-permute-start(bf16[272,256]{1,0:T(8,128)(2,1)S(1)} %get-tuple-element.77), channel_id=1, source_target_pairs={{0,4},{4,0},{8,12},{12,8},{16,20},{20,16},{24,28},{28,24},{1,5},{5... | collective-permute-start | bytes 417800 | tf_op jit(solution)/shard_map/ppermute | solution.py:47
  56.1 7.2 %collective-permute-start.13 = (bf16[272,256]{1,0:T(8,128)(2,1)S(1)}, bf16[272,256]{1,0:T(8,128)(2,1)S(1)}, u32[]{:S(2)}, u32[]{:S(2)}) collective-permute-start(bf16[272,256]{1,0:T(8,128)(2,1)S(1)} %get-tuple-element.78), channel_id=1, source_target_pairs={{0,8},{4,12},{8,0},{12,4},{16,24},{20,28},{24,16},{28,20},{1,9},{5... | collective-permute-start | bytes 417800 | tf_op jit(solution)/shard_map/ppermute | solution.py:47
  57.7 6.4 %collective-permute-start.14 = (bf16[272,256]{1,0:T(8,128)(2,1)S(1)}, bf16[272,256]{1,0:T(8,128)(2,1)S(1)}, u32[]{:S(2)}, u32[]{:S(2)}) collective-permute-start(bf16[272,256]{1,0:T(8,128)(2,1)S(1)} %get-tuple-element.79), channel_id=1, source_target_pairs={{0,12},{4,8},{8,4},{12,0},{16,28},{20,24},{24,20},{28,16},{1,13},{... | collective-permute-start | bytes 417800 | tf_op jit(solution)/shard_map/ppermute | solution.py:47
  61.7 16.3 %collective-permute-start.19 = (bf16[2,1,96,1024]{3,2,1,0:T(8,128)(2,1)S(1)}, bf16[2,1,96,1024]{3,2,1,0:T(8,128)(2,1)S(1)}, u32[]{:S(2)}, u32[]{:S(2)}) collective-permute-start(bf16[2,1,96,1024]{3,2,1,0:T(8,128)(2,1)S(1)} %get-tuple-element.85), channel_id=1, source_target_pairs={{0,2},{1,3},{2,0},{3,1},{4,6},{5,7},{6,4},{7,5},{8,10},{9,11},{10,... | collective-permute-start | bytes 1179656 | tf_op jit(solution)/shard_map/ppermute | solution.py:47
  64.7 8.9 %collective-permute-start.18 = (bf16[272,256]{1,0:T(8,128)(2,1)S(1)}, bf16[272,256]{1,0:T(8,128)(2,1)S(1)}, u32[]{:S(2)}, u32[]{:S(2)}) collective-permute-start(bf16[272,256]{1,0:T(8,128)(2,1)S(1)} %chain_step.6.refs_0_), channel_id=1, source_target_pairs={{0,16},{4,20},{8,24},{12,28},{16,0},{20,4},{24,8},{28,12},{1,17},{... | collective-permute-start | bytes 417800 | tf_op jit(solution)/shard_map/ppermute | solution.py:47
  70.9 19.2 %collective-permute-start.17 = (bf16[96,4096]{1,0:T(8,128)(2,1)S(1)}, bf16[96,4096]{1,0:T(8,128)(2,1)S(1)}, u32[]{:S(2)}, u32[]{:S(2)}) collective-permute-start(bf16[96,4096]{1,0:T(8,128)(2,1)S(1)} %get-tuple-element.82), channel_id=1, source_target_pairs={{0,2},{1,3},{2,0},{3,1},{4,6},{5,7},{6,4},{7,5},{8,10},{9,11},{10,... | collective-permute-start | bytes 2359304 | tf_op jit(solution)/shard_map/ppermute | solution.py:47
  74.5 7.0 %collective-permute-start.20 = (bf16[272,256]{1,0:T(8,128)(2,1)S(1)}, bf16[272,256]{1,0:T(8,128)(2,1)S(1)}, u32[]{:S(2)}, u32[]{:S(2)}) collective-permute-start(bf16[272,256]{1,0:T(8,128)(2,1)S(1)} %get-tuple-element.88), channel_id=1, source_target_pairs={{0,4},{4,0},{8,12},{12,8},{16,20},{20,16},{24,28},{28,24},{1,5},{5... | collective-permute-start | bytes 417800 | tf_op jit(solution)/shard_map/ppermute | solution.py:47
  76.0 5.8 %collective-permute-start.21 = (bf16[272,256]{1,0:T(8,128)(2,1)S(1)}, bf16[272,256]{1,0:T(8,128)(2,1)S(1)}, u32[]{:S(2)}, u32[]{:S(2)}) collective-permute-start(bf16[272,256]{1,0:T(8,128)(2,1)S(1)} %get-tuple-element.89), channel_id=1, source_target_pairs={{0,8},{4,12},{8,0},{12,4},{16,24},{20,28},{24,16},{28,20},{1,9},{5... | collective-permute-start | bytes 417800 | tf_op jit(solution)/shard_map/ppermute | solution.py:47
  76.7 7.3 %collective-permute-start.22 = (bf16[272,256]{1,0:T(8,128)(2,1)S(1)}, bf16[272,256]{1,0:T(8,128)(2,1)S(1)}, u32[]{:S(2)}, u32[]{:S(2)}) collective-permute-start(bf16[272,256]{1,0:T(8,128)(2,1)S(1)} %get-tuple-element.90), channel_id=1, source_target_pairs={{0,12},{4,8},{8,4},{12,0},{16,28},{20,24},{24,20},{28,16},{1,13},{... | collective-permute-start | bytes 417800 | tf_op jit(solution)/shard_map/ppermute | solution.py:47
  88.1 12.0 %collective-permute-start.24 = (bf16[96,2048]{1,0:T(8,128)(2,1)S(1)}, bf16[96,2048]{1,0:T(8,128)(2,1)S(1)}, u32[]{:S(2)}, u32[]{:S(2)}) collective-permute-start(bf16[96,2048]{1,0:T(8,128)(2,1)S(1)} %get-tuple-element.94), channel_id=1, source_target_pairs={{0,2},{1,3},{2,0},{3,1},{4,6},{5,7},{6,4},{7,5},{8,10},{9,11},{10,... | collective-permute-start | bytes 1179656 | tf_op jit(solution)/shard_map/ppermute | solution.py:47
  91.5 14.9 %collective-permute-start.25 = (bf16[96,1536]{1,0:T(8,128)(2,1)S(1)}, bf16[96,1536]{1,0:T(8,128)(2,1)S(1)}, u32[]{:S(2)}, u32[]{:S(2)}) collective-permute-start(bf16[96,1536]{1,0:T(8,128)(2,1)S(1)} %get-tuple-element.96), channel_id=1, source_target_pairs={{0,2},{1,3},{2,0},{3,1},{4,6},{5,7},{6,4},{7,5},{8,10},{9,11},{10,... | collective-permute-start | bytes 884744 | tf_op jit(solution)/shard_map/ppermute | solution.py:47
  93.7 14.1 %collective-permute-start.26 = (bf16[96,512]{1,0:T(8,128)(2,1)S(1)}, bf16[96,512]{1,0:T(8,128)(2,1)S(1)}, u32[]{:S(2)}, u32[]{:S(2)}) collective-permute-start(bf16[96,512]{1,0:T(8,128)(2,1)S(1)} %get-tuple-element.98), channel_id=1, source_target_pairs={{0,2},{1,3},{2,0},{3,1},{4,6},{5,7},{6,4},{7,5},{8,10},{9,11},{10,... | collective-permute-start | bytes 294920 | tf_op jit(solution)/shard_map/ppermute | solution.py:47
  (10 other events, 56.9 us)

commit v4 on v3

--- a/solution.py
+++ b/solution.py
@@ -634,7 +634,7 @@
     slabs = [SLABS[0]] * (seqs - 1) + [SLABS[1]]
     plan = []
     for n in range(seqs):
-        came = 22 * n
+        came = 20.9 * n
         end = came + 22 + 9 * levels
         plan.append((came, state, n))
         if n > 0:

time: 109 us -> 109 us (level)
  no operation moved by 1% of the time
where the time goes in v4:
time: 109 us
  waiting for transfers between devices  34.4 us (32%)
  Pallas kernels  32.4 us (30%)
  starting transfers between devices  31.5 us (29%)
  local copies, waits for them, and re-layouts  10.2 us (9%)
    ppermute x27, waiting for transfers between devices, swap(): lax.ppermute(value, axis, [(j, j ^ bit) for j in range(lax.axis_size(axis...  34.4 us
    ppermute x27, starting transfers between devices, swap(): lax.ppermute(value, axis, [(j, j ^ bit) for j in range(lax.axis_size(axis...  31.5 us
    unnamed x16, local copies, waits for them, and re-layouts  10.2 us
    pallas_call x3, Pallas kernels, attend_local(): pl.pallas_call(ordered(functools.partial(local_kernel, first, q_at, v_at,...  7.53 us
    pallas_call x4, Pallas kernels, project(): pl.pallas_call(ordered(functools.partial(kernel, first, math.gcd(unit, 51...  6.52 us
    pallas_call x2, Pallas kernels, pack(): pl.pallas_call(functools.partial(pack_kernel, places, len(arrays)), out_s...  4.28 us
    pallas_call x2, Pallas kernels, block_state(): pl.pallas_call(ordered(functools.partial(state_kernel, k_at, v_at, heads,...  3.09 us
    pallas_call x4, Pallas kernels, chain_step(): pl.pallas_call(ordered(functools.partial(step_kernel, levels), len(after)...  2.93 us
  transfers between devices with their start and end apart: 27, of which 14 were waited for; matrix products, arithmetic and copies ran while one was open for 7% of the time, Pallas kernels for 25%

profile of v4, /device:TPU:0, one launch (start us, length us, event | category | flops | bytes accessed | tf_op | source)
XLA Modules:
  0.0 108.8 jit_solution(10461266212200567536)
XLA Ops:
  0.0 3.3 %pack.2 = (bf16[1,2,96,1024]{3,2,1,0:T(8,128)(2,1)}, bf16[1,2,96,1024]{3,2,1,0:T(8,128)(2,1)}, bf16[1,10,96,1024]{3,2,1,0:T(8,128)(2,1)}) custom-call(bf16[2,3,96,4096]{3,2,1,0:T(8,128)(2,1)} %bitcast.8), custom_call_target="tpu_custom_call" | custom-call | tf_op jit(solution)/shard_map/pack/pallas_call | solution.py:136
  3.8 2.6 %collective-permute-start.1 = (bf16[1,2,96,1024]{3,2,1,0:T(8,128)(2,1)}, bf16[1,2,96,1024]{3,2,1,0:T(8,128)(2,1)S(1)}, u32[]{:S(2)}, u32[]{:S(2)}) collective-permute-start(bf16[1,2,96,1024]{3,2,1,0:T(8,128)(2,1)} %get-tuple-element.55), channel_id=1, source_target_pairs={{0,2},{1,3},{2,0},{3,1},{4,6},{5,7},{6,4},{7,5},{8,10},{9,11},{10,... | collective-permute-start | bytes 1179656 | tf_op jit(solution)/shard_map/ppermute | solution.py:47
  6.5 7.8 %copy.8.refs_0_ = bf16[1024,4096]{1,0:T(8,128)(2,1)} copy(bf16[1024,4096]{1,0:T(8,128)(2,1)} %refs_3_.3) | data formatting | bytes 16777216
  15.0 2.3 %copy-done = bf16[2,96,3,4096]{3,1,2,0:T(8,128)(2,1)S(1)} copy-done((bf16[2,96,3,4096]{3,1,2,0:T(8,128)(2,1)S(1)}, bf16[2,96,3,4096]{3,1,2,0:T(8,128)(2,1)}, u32[]{:S(2)}) %copy-start) | copy-done | bytes 4718616
  19.2 5.3 %collective-permute-done.2.refs_4_.refs_6_.refs_10_ = bf16[1,2,96,1024]{3,2,1,0:T(8,128)(2,1)S(1)} collective-permute-done((bf16[1,2,96,1024]{3,2,1,0:T(8,128)(2,1)}, bf16[1,2,96,1024]{3,2,1,0:T(8,128)(2,1)S(1)}, u32[]{:S(2)}, u32[]{:S(2)}) %collective-permute-start.2) | collective-permute-done | bytes 393248 | tf_op jit(solution)/shard_map/ppermute | solution.py:47
  26.3 1.7 %collective-permute-start.6 = (bf16[2,2,96,1024]{3,2,1,0:T(8,128)(2,1)S(1)}, bf16[2,2,96,1024]{3,2,1,0:T(8,128)(2,1)S(1)}, u32[]{:S(2)}, u32[]{:S(2)}) collective-permute-start(bf16[2,2,96,1024]{3,2,1,0:T(8,128)(2,1)S(1)} %get-tuple-element.65), channel_id=1, source_target_pairs={{0,2},{1,3},{2,0},{3,1},{4,6},{5,7},{6,4},{7,5},{8,10},{9,11},{10,... | collective-permute-start | bytes 2359304 | tf_op jit(solution)/shard_map/ppermute | solution.py:47
  29.5 1.6 %collective-permute-start.4 = (bf16[272,256]{1,0:T(8,128)(2,1)S(1)}, bf16[272,256]{1,0:T(8,128)(2,1)S(1)}, u32[]{:S(2)}, u32[]{:S(2)}) collective-permute-start(bf16[272,256]{1,0:T(8,128)(2,1)S(1)} %get-tuple-element.61), channel_id=1, source_target_pairs={{0,8},{4,12},{8,0},{12,4},{16,24},{20,28},{24,16},{28,20},{1,9},{5... | collective-permute-start | bytes 417800 | tf_op jit(solution)/shard_map/ppermute | solution.py:47
  34.1 2.1 %collective-permute-done.4.refs_4_ = bf16[272,256]{1,0:T(8,128)(2,1)S(1)} collective-permute-done((bf16[272,256]{1,0:T(8,128)(2,1)S(1)}, bf16[272,256]{1,0:T(8,128)(2,1)S(1)}, u32[]{:S(2)}, u32[]{:S(2)}) %collective-permute-start.4) | collective-permute-done | bytes 139296 | tf_op jit(solution)/shard_map/ppermute | solution.py:47
  36.1 1.6 %collective-permute-done.5.refs_5_ = bf16[272,256]{1,0:T(8,128)(2,1)S(1)} collective-permute-done((bf16[272,256]{1,0:T(8,128)(2,1)S(1)}, bf16[272,256]{1,0:T(8,128)(2,1)S(1)}, u32[]{:S(2)}, u32[]{:S(2)}) %collective-permute-start.5) | collective-permute-done | bytes 139296 | tf_op jit(solution)/shard_map/ppermute | solution.py:47
  38.3 2.7 %collective-permute-start.7 = (bf16[272,256]{1,0:T(8,128)(2,1)S(1)}, bf16[272,256]{1,0:T(8,128)(2,1)S(1)}, u32[]{:S(2)}, u32[]{:S(2)}) collective-permute-start(bf16[272,256]{1,0:T(8,128)(2,1)S(1)} %chain_step.4.refs_0_), channel_id=1, source_target_pairs={{0,16},{4,20},{8,24},{12,28},{16,0},{20,4},{24,8},{28,12},{1,17},{... | collective-permute-start | bytes 417800 | tf_op jit(solution)/shard_map/ppermute | solution.py:47
  41.0 2.1 %attend_local.3 = (bf16[8,192,256]{2,1,0:T(8,128)(2,1)S(1)}, f32[8,192,256]{2,1,0:T(8,128)S(1)}) custom-call(bf16[272,256]{1,0:T(8,128)(2,1)S(1)} %chain_step.4.refs_0_, s32[3]{0:T(128)S(1)} %pad_add_fusion.refs_1_, bf16[8,256,256]{2,1,0:T(8,128)(2,1)S(1)} %integer_maps.1.refs_1_.refs_2_, bf16[8,192,256]{2,1,0:T(8,128)(2,1)S(1)} %get-tuple-element.54.refs_0_.refs_3_, ...), custom_call_target="tpu_custom_call" | custom-call | flops 3000000000 | tf_op jit(solution)/shard_map/attend_local/pallas_call | solution.py:320
  43.1 3.6 %collective-permute-done.6.refs_3_.refs_4_.refs_5_.refs_6_.refs_11_.refs_12_ = bf16[2,2,96,1024]{3,2,1,0:T(8,128)(2,1)S(1)} collective-permute-done((bf16[2,2,96,1024]{3,2,1,0:T(8,128)(2,1)S(1)}, bf16[2,2,96,1024]{3,2,1,0:T(8,128)(2,1)S(1)}, u32[]{:S(2)}, u32[]{:S(2)}) %collective-permute-start.6) | collective-permute-done | bytes 786464 | tf_op jit(solution)/shard_map/ppermute | solution.py:47
  49.0 1.9 %collective-permute-start.10 = (bf16[272,256]{1,0:T(8,128)(2,1)S(1)}, bf16[272,256]{1,0:T(8,128)(2,1)S(1)}, u32[]{:S(2)}, u32[]{:S(2)}) collective-permute-start(bf16[272,256]{1,0:T(8,128)(2,1)S(1)} %get-tuple-element.74), channel_id=1, source_target_pairs={{0,8},{4,12},{8,0},{12,4},{16,24},{20,28},{24,16},{28,20},{1,9},{5... | collective-permute-start | bytes 417800 | tf_op jit(solution)/shard_map/ppermute | solution.py:47
  52.6 2.0 %collective-permute-done.8.refs_5_.refs_6_ = bf16[2,1,96,1024]{3,2,1,0:T(8,128)(2,1)S(1)} collective-permute-done((bf16[2,1,96,1024]{3,2,1,0:T(8,128)(2,1)S(1)}, bf16[2,1,96,1024]{3,2,1,0:T(8,128)(2,1)S(1)}, u32[]{:S(2)}, u32[]{:S(2)}) %collective-permute-start.8) | collective-permute-done | bytes 393248 | tf_op jit(solution)/shard_map/ppermute | solution.py:47
  59.2 2.0 %attend_local.4 = (bf16[8,192,256]{2,1,0:T(8,128)(2,1)S(1)}, f32[8,192,256]{2,1,0:T(8,128)S(1)}) custom-call(bf16[272,256]{1,0:T(8,128)(2,1)S(1)} %get-tuple-element.68.refs_0_.refs_6_, s32[3]{0:T(128)S(1)} %pad_add_fusion.refs_1_, bf16[8,256,256]{2,1,0:T(8,128)(2,1)S(1)} %integer_maps.1.refs_1_.refs_2_, ...), custom_call_target="tpu_custom_call" | custom-call | flops 3000000000 | tf_op jit(solution)/shard_map/attend_local/pallas_call | solution.py:320
  62.8 2.2 %collective-permute-done.12.refs_3_ = bf16[272,256]{1,0:T(8,128)(2,1)S(1)} collective-permute-done((bf16[272,256]{1,0:T(8,128)(2,1)S(1)}, bf16[272,256]{1,0:T(8,128)(2,1)S(1)}, u32[]{:S(2)}, u32[]{:S(2)}) %collective-permute-start.12) | collective-permute-done | bytes 139296 | tf_op jit(solution)/shard_map/ppermute | solution.py:47
  67.1 2.6 %collective-permute-start.18 = (bf16[272,256]{1,0:T(8,128)(2,1)S(1)}, bf16[272,256]{1,0:T(8,128)(2,1)S(1)}, u32[]{:S(2)}, u32[]{:S(2)}) collective-permute-start(bf16[272,256]{1,0:T(8,128)(2,1)S(1)} %chain_step.6.refs_0_), channel_id=1, source_target_pairs={{0,16},{4,20},{8,24},{12,28},{16,0},{20,4},{24,8},{28,12},{1,17},{... | collective-permute-start | bytes 417800 | tf_op jit(solution)/shard_map/ppermute | solution.py:47
  69.8 3.5 %project.4 = (f32[96,4096]{1,0:T(8,128)S(1)}, bf16[96,4096]{1,0:T(8,128)(2,1)S(1)}) custom-call(bf16[272,256]{1,0:T(8,128)(2,1)S(1)} %chain_step.6.refs_0_, bf16[2,96,1024]{2,1,0:T(8,128)(2,1)S(1)} %get-tuple-element.76.refs_0_.refs_1_, bf16[2,96,1024]{2,1,0:T(8,128)(2,1)S(1)} %collective-permute-done.15.refs_2_, bf16[1024,4096]{1,0:T(8,128)(2,1)S(1)} %bitcast.5, ...), custom_call_target="tpu_custom_call" | custom-call | flops 6000000000 | tf_op jit(solution)/shard_map/project/pallas_call | solution.py:434
  77.1 2.2 %collective-permute-start.22 = (bf16[272,256]{1,0:T(8,128)(2,1)S(1)}, bf16[272,256]{1,0:T(8,128)(2,1)S(1)}, u32[]{:S(2)}, u32[]{:S(2)}) collective-permute-start(bf16[272,256]{1,0:T(8,128)(2,1)S(1)} %get-tuple-element.90), channel_id=1, source_target_pairs={{0,12},{4,8},{8,4},{12,0},{16,28},{20,24},{24,20},{28,16},{1,13},{... | collective-permute-start | bytes 417800 | tf_op jit(solution)/shard_map/ppermute | solution.py:47
  79.3 3.4 %attend_local.5 = (bf16[8,384,256]{2,1,0:T(8,128)(2,1)S(1)}, f32[8,384,256]{2,1,0:T(8,128)S(1)}) custom-call(bf16[272,256]{1,0:T(8,128)(2,1)S(1)} %get-tuple-element.83.refs_0_.refs_4_, s32[3]{0:T(128)S(1)} %pad_add_fusion.refs_1_, bf16[8,256,256]{2,1,0:T(8,128)(2,1)S(1)} %integer_maps.1.refs_1_.refs_2_, ...), custom_call_target="tpu_custom_call" | custom-call | flops 3000000000 | tf_op jit(solution)/shard_map/attend_local/pallas_call | solution.py:320
  89.1 2.1 %collective-permute-done.17.refs_1_ = bf16[96,4096]{1,0:T(8,128)(2,1)S(1)} collective-permute-done((bf16[96,4096]{1,0:T(8,128)(2,1)S(1)}, bf16[96,4096]{1,0:T(8,128)(2,1)S(1)}, u32[]{:S(2)}, u32[]{:S(2)}) %collective-permute-start.17) | collective-permute-done | bytes 786464 | tf_op jit(solution)/shard_map/ppermute | solution.py:47
  92.6 2.4 %collective-permute-start.25 = (bf16[96,1536]{1,0:T(8,128)(2,1)S(1)}, bf16[96,1536]{1,0:T(8,128)(2,1)S(1)}, u32[]{:S(2)}, u32[]{:S(2)}) collective-permute-start(bf16[96,1536]{1,0:T(8,128)(2,1)S(1)} %get-tuple-element.96), channel_id=1, source_target_pairs={{0,2},{1,3},{2,0},{3,1},{4,6},{5,7},{6,4},{7,5},{8,10},{9,11},{10,... | collective-permute-start | bytes 884744 | tf_op jit(solution)/shard_map/ppermute | solution.py:47
  95.8 4.7 %collective-permute-done.24.refs_3_ = bf16[96,2048]{1,0:T(8,128)(2,1)S(1)} collective-permute-done((bf16[96,2048]{1,0:T(8,128)(2,1)S(1)}, bf16[96,2048]{1,0:T(8,128)(2,1)S(1)}, u32[]{:S(2)}, u32[]{:S(2)}) %collective-permute-start.24) | collective-permute-done | bytes 393248 | tf_op jit(solution)/shard_map/ppermute | solution.py:47
  100.5 6.3 %collective-permute-done.25.refs_5_ = bf16[96,1536]{1,0:T(8,128)(2,1)S(1)} collective-permute-done((bf16[96,1536]{1,0:T(8,128)(2,1)S(1)}, bf16[96,1536]{1,0:T(8,128)(2,1)S(1)}, u32[]{:S(2)}, u32[]{:S(2)}) %collective-permute-start.25) | collective-permute-done | bytes 294944 | tf_op jit(solution)/shard_map/ppermute | solution.py:47
  (73 shorter events, 36.5 us)
Async XLA Ops:
  3.3 11.6 %collective-permute-start = (bf16[1,10,96,1024]{3,2,1,0:T(8,128)(2,1)}, bf16[1,10,96,1024]{3,2,1,0:T(8,128)(2,1)S(1)}, u32[]{:S(2)}, u32[]{:S(2)}) collective-permute-start(bf16[1,10,96,1024]{3,2,1,0:T(8,128)(2,1)} %get-tuple-element.52), channel_id=1, source_target_pairs={{0,1},{1,0},{2,3},{3,2},{4,5},{5,4},{6,7},{7,6},{8,9},{9,8},{10,11... | collective-permute-start | bytes 5898248 | tf_op jit(solution)/shard_map/ppermute | solution.py:47
  3.8 15.4 %collective-permute-start.1 = (bf16[1,2,96,1024]{3,2,1,0:T(8,128)(2,1)}, bf16[1,2,96,1024]{3,2,1,0:T(8,128)(2,1)S(1)}, u32[]{:S(2)}, u32[]{:S(2)}) collective-permute-start(bf16[1,2,96,1024]{3,2,1,0:T(8,128)(2,1)} %get-tuple-element.55), channel_id=1, source_target_pairs={{0,2},{1,3},{2,0},{3,1},{4,6},{5,7},{6,4},{7,5},{8,10},{9,11},{10,... | collective-permute-start | bytes 1179656 | tf_op jit(solution)/shard_map/ppermute | solution.py:47
  6.4 18.1 %collective-permute-start.2 = (bf16[1,2,96,1024]{3,2,1,0:T(8,128)(2,1)}, bf16[1,2,96,1024]{3,2,1,0:T(8,128)(2,1)S(1)}, u32[]{:S(2)}, u32[]{:S(2)}) collective-permute-start(bf16[1,2,96,1024]{3,2,1,0:T(8,128)(2,1)} %get-tuple-element.56), channel_id=1, source_target_pairs={{0,3},{1,2},{2,1},{3,0},{4,7},{5,6},{6,5},{7,4},{8,11},{9,10},{10,... | collective-permute-start | bytes 1179656 | tf_op jit(solution)/shard_map/ppermute | solution.py:47
  26.1 43.7 %collective-permute-start.16 = (bf16[1024,4096]{1,0:T(8,128)(2,1)S(1)}, bf16[1024,4096]{1,0:T(8,128)(2,1)S(1)}, u32[]{:S(2)}, u32[]{:S(2)}) collective-permute-start(bf16[1024,4096]{1,0:T(8,128)(2,1)S(1)} %later_than.1), channel_id=1, source_target_pairs={{0,1},{1,0},{2,3},{3,2},{4,5},{5,4},{6,7},{7,6},{8,9},{9,8},{10,11... | collective-permute-start | bytes 25165832 | tf_op jit(solution)/shard_map/ppermute | solution.py:47
  26.3 20.3 %collective-permute-start.6 = (bf16[2,2,96,1024]{3,2,1,0:T(8,128)(2,1)S(1)}, bf16[2,2,96,1024]{3,2,1,0:T(8,128)(2,1)S(1)}, u32[]{:S(2)}, u32[]{:S(2)}) collective-permute-start(bf16[2,2,96,1024]{3,2,1,0:T(8,128)(2,1)S(1)} %get-tuple-element.65), channel_id=1, source_target_pairs={{0,2},{1,3},{2,0},{3,1},{4,6},{5,7},{6,4},{7,5},{8,10},{9,11},{10,... | collective-permute-start | bytes 2359304 | tf_op jit(solution)/shard_map/ppermute | solution.py:47
  29.5 6.6 %collective-permute-start.4 = (bf16[272,256]{1,0:T(8,128)(2,1)S(1)}, bf16[272,256]{1,0:T(8,128)(2,1)S(1)}, u32[]{:S(2)}, u32[]{:S(2)}) collective-permute-start(bf16[272,256]{1,0:T(8,128)(2,1)S(1)} %get-tuple-element.61), channel_id=1, source_target_pairs={{0,8},{4,12},{8,0},{12,4},{16,24},{20,28},{24,16},{28,20},{1,9},{5... | collective-permute-start | bytes 417800 | tf_op jit(solution)/shard_map/ppermute | solution.py:47
  31.1 6.6 %collective-permute-start.5 = (bf16[272,256]{1,0:T(8,128)(2,1)S(1)}, bf16[272,256]{1,0:T(8,128)(2,1)S(1)}, u32[]{:S(2)}, u32[]{:S(2)}) collective-permute-start(bf16[272,256]{1,0:T(8,128)(2,1)S(1)} %get-tuple-element.62), channel_id=1, source_target_pairs={{0,12},{4,8},{8,4},{12,0},{16,28},{20,24},{24,20},{28,16},{1,13},{... | collective-permute-start | bytes 417800 | tf_op jit(solution)/shard_map/ppermute | solution.py:47
  33.6 21.0 %collective-permute-start.8 = (bf16[2,1,96,1024]{3,2,1,0:T(8,128)(2,1)S(1)}, bf16[2,1,96,1024]{3,2,1,0:T(8,128)(2,1)S(1)}, u32[]{:S(2)}, u32[]{:S(2)}) collective-permute-start(bf16[2,1,96,1024]{3,2,1,0:T(8,128)(2,1)S(1)} %get-tuple-element.69), channel_id=1, source_target_pairs={{0,2},{1,3},{2,0},{3,1},{4,6},{5,7},{6,4},{7,5},{8,10},{9,11},{10,... | collective-permute-start | bytes 1179656 | tf_op jit(solution)/shard_map/ppermute | solution.py:47
  38.3 9.8 %collective-permute-start.7 = (bf16[272,256]{1,0:T(8,128)(2,1)S(1)}, bf16[272,256]{1,0:T(8,128)(2,1)S(1)}, u32[]{:S(2)}, u32[]{:S(2)}) collective-permute-start(bf16[272,256]{1,0:T(8,128)(2,1)S(1)} %chain_step.4.refs_0_), channel_id=1, source_target_pairs={{0,16},{4,20},{8,24},{12,28},{16,0},{20,4},{24,8},{28,12},{1,17},{... | collective-permute-start | bytes 417800 | tf_op jit(solution)/shard_map/ppermute | solution.py:47
  49.0 7.1 %collective-permute-start.10 = (bf16[272,256]{1,0:T(8,128)(2,1)S(1)}, bf16[272,256]{1,0:T(8,128)(2,1)S(1)}, u32[]{:S(2)}, u32[]{:S(2)}) collective-permute-start(bf16[272,256]{1,0:T(8,128)(2,1)S(1)} %get-tuple-element.74), channel_id=1, source_target_pairs={{0,8},{4,12},{8,0},{12,4},{16,24},{20,28},{24,16},{28,20},{1,9},{5... | collective-permute-start | bytes 417800 | tf_op jit(solution)/shard_map/ppermute | solution.py:47
  50.9 6.8 %collective-permute-start.11 = (bf16[272,256]{1,0:T(8,128)(2,1)S(1)}, bf16[272,256]{1,0:T(8,128)(2,1)S(1)}, u32[]{:S(2)}, u32[]{:S(2)}) collective-permute-start(bf16[272,256]{1,0:T(8,128)(2,1)S(1)} %get-tuple-element.75), channel_id=1, source_target_pairs={{0,12},{4,8},{8,4},{12,0},{16,28},{20,24},{24,20},{28,16},{1,13},{... | collective-permute-start | bytes 417800 | tf_op jit(solution)/shard_map/ppermute | solution.py:47
  52.3 9.0 %collective-permute-start.9 = (bf16[272,256]{1,0:T(8,128)(2,1)S(1)}, bf16[272,256]{1,0:T(8,128)(2,1)S(1)}, u32[]{:S(2)}, u32[]{:S(2)}) collective-permute-start(bf16[272,256]{1,0:T(8,128)(2,1)S(1)} %get-tuple-element.73), channel_id=1, source_target_pairs={{0,4},{4,0},{8,12},{12,8},{16,20},{20,16},{24,28},{28,24},{1,5},{5... | collective-permute-start | bytes 417800 | tf_op jit(solution)/shard_map/ppermute | solution.py:47
  54.6 10.4 %collective-permute-start.12 = (bf16[272,256]{1,0:T(8,128)(2,1)S(1)}, bf16[272,256]{1,0:T(8,128)(2,1)S(1)}, u32[]{:S(2)}, u32[]{:S(2)}) collective-permute-start(bf16[272,256]{1,0:T(8,128)(2,1)S(1)} %get-tuple-element.77), channel_id=1, source_target_pairs={{0,4},{4,0},{8,12},{12,8},{16,20},{20,16},{24,28},{28,24},{1,5},{5... | collective-permute-start | bytes 417800 | tf_op jit(solution)/shard_map/ppermute | solution.py:47
  56.1 10.4 %collective-permute-start.13 = (bf16[272,256]{1,0:T(8,128)(2,1)S(1)}, bf16[272,256]{1,0:T(8,128)(2,1)S(1)}, u32[]{:S(2)}, u32[]{:S(2)}) collective-permute-start(bf16[272,256]{1,0:T(8,128)(2,1)S(1)} %get-tuple-element.78), channel_id=1, source_target_pairs={{0,8},{4,12},{8,0},{12,4},{16,24},{20,28},{24,16},{28,20},{1,9},{5... | collective-permute-start | bytes 417800 | tf_op jit(solution)/shard_map/ppermute | solution.py:47
  57.7 8.8 %collective-permute-start.14 = (bf16[272,256]{1,0:T(8,128)(2,1)S(1)}, bf16[272,256]{1,0:T(8,128)(2,1)S(1)}, u32[]{:S(2)}, u32[]{:S(2)}) collective-permute-start(bf16[272,256]{1,0:T(8,128)(2,1)S(1)} %get-tuple-element.79), channel_id=1, source_target_pairs={{0,12},{4,8},{8,4},{12,0},{16,28},{20,24},{24,20},{28,16},{1,13},{... | collective-permute-start | bytes 417800 | tf_op jit(solution)/shard_map/ppermute | solution.py:47
  62.8 7.0 %collective-permute-start.15 = (bf16[2,96,1024]{2,1,0:T(8,128)(2,1)S(1)}, bf16[2,96,1024]{2,1,0:T(8,128)(2,1)S(1)}, u32[]{:S(2)}, u32[]{:S(2)}) collective-permute-start(bf16[2,96,1024]{2,1,0:T(8,128)(2,1)S(1)} %get-tuple-element.80), channel_id=1, source_target_pairs={{0,1},{1,0},{2,3},{3,2},{4,5},{5,4},{6,7},{7,6},{8,9},{9,8},{10,11... | collective-permute-start | bytes 1179656 | tf_op jit(solution)/shard_map/ppermute | solution.py:47
  65.0 14.3 %collective-permute-start.19 = (bf16[2,1,96,1024]{3,2,1,0:T(8,128)(2,1)S(1)}, bf16[2,1,96,1024]{3,2,1,0:T(8,128)(2,1)S(1)}, u32[]{:S(2)}, u32[]{:S(2)}) collective-permute-start(bf16[2,1,96,1024]{3,2,1,0:T(8,128)(2,1)S(1)} %get-tuple-element.85), channel_id=1, source_target_pairs={{0,2},{1,3},{2,0},{3,1},{4,6},{5,7},{6,4},{7,5},{8,10},{9,11},{10,... | collective-permute-start | bytes 1179656 | tf_op jit(solution)/shard_map/ppermute | solution.py:47
  67.1 7.7 %collective-permute-start.18 = (bf16[272,256]{1,0:T(8,128)(2,1)S(1)}, bf16[272,256]{1,0:T(8,128)(2,1)S(1)}, u32[]{:S(2)}, u32[]{:S(2)}) collective-permute-start(bf16[272,256]{1,0:T(8,128)(2,1)S(1)} %chain_step.6.refs_0_), channel_id=1, source_target_pairs={{0,16},{4,20},{8,24},{12,28},{16,0},{20,4},{24,8},{28,12},{1,17},{... | collective-permute-start | bytes 417800 | tf_op jit(solution)/shard_map/ppermute | solution.py:47
  73.3 17.9 %collective-permute-start.17 = (bf16[96,4096]{1,0:T(8,128)(2,1)S(1)}, bf16[96,4096]{1,0:T(8,128)(2,1)S(1)}, u32[]{:S(2)}, u32[]{:S(2)}) collective-permute-start(bf16[96,4096]{1,0:T(8,128)(2,1)S(1)} %get-tuple-element.82), channel_id=1, source_target_pairs={{0,2},{1,3},{2,0},{3,1},{4,6},{5,7},{6,4},{7,5},{8,10},{9,11},{10,... | collective-permute-start | bytes 2359304 | tf_op jit(solution)/shard_map/ppermute | solution.py:47
  75.7 7.0 %collective-permute-start.20 = (bf16[272,256]{1,0:T(8,128)(2,1)S(1)}, bf16[272,256]{1,0:T(8,128)(2,1)S(1)}, u32[]{:S(2)}, u32[]{:S(2)}) collective-permute-start(bf16[272,256]{1,0:T(8,128)(2,1)S(1)} %get-tuple-element.88), channel_id=1, source_target_pairs={{0,4},{4,0},{8,12},{12,8},{16,20},{20,16},{24,28},{28,24},{1,5},{5... | collective-permute-start | bytes 417800 | tf_op jit(solution)/shard_map/ppermute | solution.py:47
  77.1 7.3 %collective-permute-start.22 = (bf16[272,256]{1,0:T(8,128)(2,1)S(1)}, bf16[272,256]{1,0:T(8,128)(2,1)S(1)}, u32[]{:S(2)}, u32[]{:S(2)}) collective-permute-start(bf16[272,256]{1,0:T(8,128)(2,1)S(1)} %get-tuple-element.90), channel_id=1, source_target_pairs={{0,12},{4,8},{8,4},{12,0},{16,28},{20,24},{24,20},{28,16},{1,13},{... | collective-permute-start | bytes 417800 | tf_op jit(solution)/shard_map/ppermute | solution.py:47
  88.5 12.0 %collective-permute-start.24 = (bf16[96,2048]{1,0:T(8,128)(2,1)S(1)}, bf16[96,2048]{1,0:T(8,128)(2,1)S(1)}, u32[]{:S(2)}, u32[]{:S(2)}) collective-permute-start(bf16[96,2048]{1,0:T(8,128)(2,1)S(1)} %get-tuple-element.94), channel_id=1, source_target_pairs={{0,2},{1,3},{2,0},{3,1},{4,6},{5,7},{6,4},{7,5},{8,10},{9,11},{10,... | collective-permute-start | bytes 1179656 | tf_op jit(solution)/shard_map/ppermute | solution.py:47
  92.6 14.2 %collective-permute-start.25 = (bf16[96,1536]{1,0:T(8,128)(2,1)S(1)}, bf16[96,1536]{1,0:T(8,128)(2,1)S(1)}, u32[]{:S(2)}, u32[]{:S(2)}) collective-permute-start(bf16[96,1536]{1,0:T(8,128)(2,1)S(1)} %get-tuple-element.96), channel_id=1, source_target_pairs={{0,2},{1,3},{2,0},{3,1},{4,6},{5,7},{6,4},{7,5},{8,10},{9,11},{10,... | collective-permute-start | bytes 884744 | tf_op jit(solution)/shard_map/ppermute | solution.py:47
  95.7 12.5 %collective-permute-start.26 = (bf16[96,512]{1,0:T(8,128)(2,1)S(1)}, bf16[96,512]{1,0:T(8,128)(2,1)S(1)}, u32[]{:S(2)}, u32[]{:S(2)}) collective-permute-start(bf16[96,512]{1,0:T(8,128)(2,1)S(1)} %get-tuple-element.98), channel_id=1, source_target_pairs={{0,2},{1,3},{2,0},{3,1},{4,6},{5,7},{6,4},{7,5},{8,10},{9,11},{10,... | collective-permute-start | bytes 294920 | tf_op jit(solution)/shard_map/ppermute | solution.py:47
  (10 other events, 58.4 us)
